TPU v7x, 32 devices: a whole 2x2x4 slice. The times are simulated.
32 devices in a mesh: rep: 8 (over z, y), shard: 4 (over x, core).
Axes of the slice: x: 2, y: 2, z: 4, core: 2. Of those that a mesh axis runs over, the one named last changes fastest.
Arguments:
- block_input: bfloat16 [8, 1024, 1088], P('rep', 'shard'), may hold values from -6 to 6
- first_gain: bfloat16 [1088], P('shard'), may hold values from 0.5 to 1.5
- first_shift: bfloat16 [1088], P('shard'), may hold values from -4 to 4
- query_key_value_weight: bfloat16 [1088, 3264], P('shard'), may hold values from -0.1875 to 0.1875
- query_bias: bfloat16 [1088], P('shard'), may hold values from -4 to 4
- value_bias: bfloat16 [1088], P('shard'), may hold values from -4 to 4
- attention_output_weight: bfloat16 [1088, 1088], P('shard'), may hold values from -0.75 to 0.75
- attention_output_bias: bfloat16 [1088], P('shard'), may hold values from -4 to 4
- second_gain: bfloat16 [1088], P('shard'), may hold values from 0.5 to 1.5
- second_shift: bfloat16 [1088], P('shard'), may hold values from -4 to 4
- up_weight: bfloat16 [1088, 4352], P('shard'), may hold values from -0.1875 to 0.1875
- up_bias: bfloat16 [4352], P('shard'), may hold values from -6 to 6
- down_weight: bfloat16 [4352, 1088], P('shard'), may hold values from -0.09375 to 0.09375
- down_bias: bfloat16 [1088], P('shard'), may hold values from -4 to 4
- cotangent: float32 [8, 1024, 1088], P('rep', 'shard'), may hold values from -8 to 8
Outputs:
- block_output: float32 [8, 1024, 1088], P('rep', 'shard')
- input_grad: float32 [8, 1024, 1088], P('rep', 'shard')
- first_gain_grad: float32 [1088], P('shard')
- first_shift_grad: float32 [1088], P('shard')
- input_weight_grad: float32 [1088, 3264], P('shard')
- query_bias_grad: float32 [1088], P('shard')
- value_bias_grad: float32 [1088], P('shard')
- output_weight_grad: float32 [1088, 1088], P('shard')
- output_bias_grad: float32 [1088], P('shard')
- second_gain_grad: float32 [1088], P('shard')
- second_shift_grad: float32 [1088], P('shard')
- up_weight_grad: float32 [1088, 4352], P('shard')
- up_bias_grad: float32 [4352], P('shard')
- down_weight_grad: float32 [4352, 1088], P('shard')
- down_bias_grad: float32 [1088], P('shard')
All inputs are finite; a program needn't handle non-finite values.
Results may differ from a plain program's by a relative error of at most 0.017.
Values may be sent and summed in bfloat16 or wider, within the bound.
No kernel may reach another device: no remote copies, remote signals or barrier semaphores. Data moves between devices by JAX's collectives and lax.ppermute only.
A program may use at most 192 MiB of HBM per device.

v0:
```python
import jax
import jax.numpy as jnp
from jax import lax
from jax.sharding import PartitionSpec as P

HEADS = 17


epsilon = 1e-05
score_scale = 0.125


def normalize(values):
    centre = jnp.mean(values, axis=-1, keepdims=True)
    centred = values - centre
    inverse = lax.rsqrt(jnp.mean(centred * centred, axis=-1, keepdims=True) + epsilon)
    return (centred * inverse, inverse)


def norm_back(grad, normed, inverse, gain):
    scaled = grad * gain
    first = jnp.mean(scaled, axis=-1, keepdims=True)
    second = jnp.mean(scaled * normed, axis=-1, keepdims=True)
    return inverse * (scaled - first - normed * second)


def gelu_slope(values):
    cumulative = 0.5 * (1.0 + lax.erf(values * 0.7071067811865476))
    density = jnp.exp(-0.5 * values * values) * 0.3989422804014327
    return cumulative + values * density


def matmul(left, right):
    return jnp.dot(left, right, preferred_element_type=jnp.float32)


def contract_rows(left, right):
    return lax.dot_general(
        left, right, (((0,), (0,)), ((), ())), preferred_element_type=jnp.float32
    )


def contract_cols(left, right):
    return lax.dot_general(
        left, right, (((1,), (1,)), ((), ())), preferred_element_type=jnp.float32
    )


def split_heads(values):
    seqs, length, width = values.shape
    return values.reshape(seqs, length, HEADS, width // HEADS).transpose(2, 0, 1, 3)


def merge_heads(values):
    heads, seqs, length, size = values.shape
    return values.transpose(1, 2, 0, 3).reshape(seqs, length, heads * size)


def local(
    block_input,
    first_gain,
    first_shift,
    query_key_value_weight,
    query_bias,
    value_bias,
    attention_output_weight,
    attention_output_bias,
    second_gain,
    second_shift,
    up_weight,
    up_bias,
    down_weight,
    down_bias,
    cotangent,
):
    seqs, span, width = block_input.shape
    rows = seqs * span
    length = span * lax.axis_size("shard")
    offset = lax.axis_index("shard") * span
    own_pos = offset + jnp.arange(span)
    all_pos = jnp.arange(length)
    visible = own_pos[:, None] >= all_pos[None, :]
    mixer_full = (
        lax.all_gather(first_gain, "shard", axis=0, tiled=True),
        lax.all_gather(first_shift, "shard", axis=0, tiled=True),
        lax.all_gather(query_key_value_weight, "shard", axis=0, tiled=True),
        lax.all_gather(query_bias, "shard", axis=0, tiled=True),
        lax.all_gather(value_bias, "shard", axis=0, tiled=True),
        lax.all_gather(attention_output_weight, "shard", axis=0, tiled=True),
        lax.all_gather(attention_output_bias, "shard", axis=0, tiled=True),
    )
    gain_one, shift_one, weight_in, bias_query, bias_value, weight_out, bias_out = mixer_full
    layer_input = block_input.reshape(rows, width).astype(jnp.float32)
    normed_one, inverse_one = normalize(layer_input)
    first_residual = (normed_one * gain_one + shift_one).astype(jnp.bfloat16)
    attention_projected = matmul(first_residual, weight_in)
    queries = (
        (attention_projected[:, :width] + bias_query)
        .astype(jnp.bfloat16)
        .reshape(seqs, span, width)
    )
    keys = attention_projected[:, width : 2 * width].astype(jnp.bfloat16).reshape(seqs, span, width)
    values = (
        (attention_projected[:, 2 * width :] + bias_value)
        .astype(jnp.bfloat16)
        .reshape(seqs, span, width)
    )
    keys_all, values_all = (
        lax.all_gather(keys, "shard", axis=1, tiled=True),
        lax.all_gather(values, "shard", axis=1, tiled=True),
    )
    heads_query = split_heads(queries)
    heads_key = split_heads(keys_all)
    heads_value = split_heads(values_all)

    def head_forward(parts):
        head_query, head_key, head_value = parts
        scores = (
            jnp.einsum("sce,sle->scl", head_query, head_key, preferred_element_type=jnp.float32)
            * score_scale
        )
        scores = jnp.where(visible, scores, -jnp.inf)
        top = jnp.max(scores, axis=-1, keepdims=True)
        log_total = top + jnp.log(jnp.sum(jnp.exp(scores - top), axis=-1, keepdims=True))
        weights_low = jnp.exp(scores - log_total).astype(jnp.bfloat16)
        mixed = jnp.einsum(
            "scl,sle->sce", weights_low, head_value, preferred_element_type=jnp.float32
        )
        return (mixed, log_total)

    mixed_heads, log_totals = lax.map(head_forward, (heads_query, heads_key, heads_value))
    attention_context = merge_heads(mixed_heads).astype(jnp.bfloat16).reshape(rows, width)
    residual_middle = layer_input + matmul(attention_context, weight_out) + bias_out
    dense_full = (
        lax.all_gather(second_gain, "shard", axis=0, tiled=True),
        lax.all_gather(second_shift, "shard", axis=0, tiled=True),
        lax.all_gather(up_weight, "shard", axis=0, tiled=True),
        lax.all_gather(up_bias, "shard", axis=0, tiled=True),
        lax.all_gather(down_weight, "shard", axis=0, tiled=True),
        lax.all_gather(down_bias, "shard", axis=0, tiled=True),
    )
    gain_two, shift_two, weight_up, bias_up, weight_down, bias_down = dense_full
    normed_two, inverse_two = normalize(residual_middle)
    hidden_two = (normed_two * gain_two + shift_two).astype(jnp.bfloat16)
    before = matmul(hidden_two, weight_up) + bias_up
    activated = jax.nn.gelu(before, approximate=False).astype(jnp.bfloat16)
    block_output = residual_middle + matmul(activated, weight_down) + bias_down
    dense_back = (
        lax.all_gather(second_gain, "shard", axis=0, tiled=True),
        lax.all_gather(second_shift, "shard", axis=0, tiled=True),
        lax.all_gather(up_weight, "shard", axis=0, tiled=True),
        lax.all_gather(up_bias, "shard", axis=0, tiled=True),
        lax.all_gather(down_weight, "shard", axis=0, tiled=True),
        lax.all_gather(down_bias, "shard", axis=0, tiled=True),
    )
    grad_out = cotangent.reshape(rows, width)
    grad_branch = grad_out.astype(jnp.bfloat16)
    down_weight_grad = contract_rows(activated, grad_branch)
    down_bias_grad = jnp.sum(grad_branch.astype(jnp.float32), axis=0)
    grad_act = contract_cols(grad_branch, dense_back[4])
    grad_before = (grad_act * gelu_slope(before)).astype(jnp.bfloat16)
    up_weight_grad = contract_rows(hidden_two, grad_before)
    up_bias_grad = jnp.sum(grad_before.astype(jnp.float32), axis=0)
    grad_hidden_two = contract_cols(grad_before, dense_back[2])
    second_gain_grad = jnp.sum(grad_hidden_two * normed_two, axis=0)
    second_shift_grad = jnp.sum(grad_hidden_two, axis=0)
    grad_middle = grad_out + norm_back(grad_hidden_two, normed_two, inverse_two, dense_back[0])
    dense_grads = (
        lax.psum_scatter(
            second_gain_grad.astype(jnp.bfloat16), "shard", scatter_dimension=0, tiled=True
        ).astype(jnp.float32),
        lax.psum_scatter(
            second_shift_grad.astype(jnp.bfloat16), "shard", scatter_dimension=0, tiled=True
        ).astype(jnp.float32),
        lax.psum_scatter(
            up_weight_grad.astype(jnp.bfloat16), "shard", scatter_dimension=0, tiled=True
        ).astype(jnp.float32),
        lax.psum_scatter(
            up_bias_grad.astype(jnp.bfloat16), "shard", scatter_dimension=0, tiled=True
        ).astype(jnp.float32),
        lax.psum_scatter(
            down_weight_grad.astype(jnp.bfloat16), "shard", scatter_dimension=0, tiled=True
        ).astype(jnp.float32),
        lax.psum_scatter(
            down_bias_grad.astype(jnp.bfloat16), "shard", scatter_dimension=0, tiled=True
        ).astype(jnp.float32),
    )
    mixer_back = (
        lax.all_gather(first_gain, "shard", axis=0, tiled=True),
        lax.all_gather(first_shift, "shard", axis=0, tiled=True),
        lax.all_gather(query_key_value_weight, "shard", axis=0, tiled=True),
        lax.all_gather(query_bias, "shard", axis=0, tiled=True),
        lax.all_gather(value_bias, "shard", axis=0, tiled=True),
        lax.all_gather(attention_output_weight, "shard", axis=0, tiled=True),
        lax.all_gather(attention_output_bias, "shard", axis=0, tiled=True),
    )
    keys_back, values_back = (
        lax.all_gather(keys, "shard", axis=1, tiled=True),
        lax.all_gather(values, "shard", axis=1, tiled=True),
    )
    heads_key = split_heads(keys_back)
    heads_value = split_heads(values_back)
    grad_mixed = grad_middle.astype(jnp.bfloat16)
    output_weight_grad = contract_rows(attention_context, grad_mixed)
    output_bias_grad = jnp.sum(grad_mixed.astype(jnp.float32), axis=0)
    grad_attended = (
        contract_cols(grad_mixed, mixer_back[5]).astype(jnp.bfloat16).reshape(seqs, span, width)
    )
    heads_grad = split_heads(grad_attended)

    def head_back(parts):
        head_query, head_key, head_value, head_grad, log_total = parts
        scores = (
            jnp.einsum("sce,sle->scl", head_query, head_key, preferred_element_type=jnp.float32)
            * score_scale
        )
        probs = jnp.exp(jnp.where(visible, scores, -jnp.inf) - log_total)
        grad_probs = jnp.einsum(
            "sce,sle->scl", head_grad, head_value, preferred_element_type=jnp.float32
        )
        value_part = jnp.einsum(
            "scl,sce->sle",
            probs.astype(jnp.bfloat16),
            head_grad,
            preferred_element_type=jnp.float32,
        )
        correction = jnp.sum(probs * grad_probs, axis=-1, keepdims=True)
        grad_scores = (probs * (grad_probs - correction)).astype(jnp.bfloat16)
        query_part = (
            jnp.einsum("scl,sle->sce", grad_scores, head_key, preferred_element_type=jnp.float32)
            * score_scale
        )
        key_part = (
            jnp.einsum("scl,sce->sle", grad_scores, head_query, preferred_element_type=jnp.float32)
            * score_scale
        )
        return (query_part, key_part, value_part)

    query_heads, key_heads, value_heads = lax.map(
        head_back, (heads_query, heads_key, heads_value, heads_grad, log_totals)
    )
    key_grad, value_grad = (
        lax.psum_scatter(
            merge_heads(key_heads).astype(jnp.bfloat16), "shard", scatter_dimension=1, tiled=True
        ).astype(jnp.float32),
        lax.psum_scatter(
            merge_heads(value_heads).astype(jnp.bfloat16), "shard", scatter_dimension=1, tiled=True
        ).astype(jnp.float32),
    )
    query_low = merge_heads(query_heads).reshape(rows, width).astype(jnp.bfloat16)
    key_low = key_grad.reshape(rows, width).astype(jnp.bfloat16)
    value_low = value_grad.reshape(rows, width).astype(jnp.bfloat16)
    grad_projected = jnp.concatenate([query_low, key_low, value_low], axis=1)
    input_weight_grad = contract_rows(first_residual, grad_projected)
    query_bias_grad = jnp.sum(query_low.astype(jnp.float32), axis=0)
    value_bias_grad = jnp.sum(value_low.astype(jnp.float32), axis=0)
    grad_hidden_one = contract_cols(grad_projected, mixer_back[2])
    first_gain_grad = jnp.sum(grad_hidden_one * normed_one, axis=0)
    first_shift_grad = jnp.sum(grad_hidden_one, axis=0)
    input_grad = grad_middle + norm_back(grad_hidden_one, normed_one, inverse_one, mixer_back[0])
    mixer_grads = (
        lax.psum_scatter(
            first_gain_grad.astype(jnp.bfloat16), "shard", scatter_dimension=0, tiled=True
        ).astype(jnp.float32),
        lax.psum_scatter(
            first_shift_grad.astype(jnp.bfloat16), "shard", scatter_dimension=0, tiled=True
        ).astype(jnp.float32),
        lax.psum_scatter(
            input_weight_grad.astype(jnp.bfloat16), "shard", scatter_dimension=0, tiled=True
        ).astype(jnp.float32),
        lax.psum_scatter(
            query_bias_grad.astype(jnp.bfloat16), "shard", scatter_dimension=0, tiled=True
        ).astype(jnp.float32),
        lax.psum_scatter(
            value_bias_grad.astype(jnp.bfloat16), "shard", scatter_dimension=0, tiled=True
        ).astype(jnp.float32),
        lax.psum_scatter(
            output_weight_grad.astype(jnp.bfloat16), "shard", scatter_dimension=0, tiled=True
        ).astype(jnp.float32),
        lax.psum_scatter(
            output_bias_grad.astype(jnp.bfloat16), "shard", scatter_dimension=0, tiled=True
        ).astype(jnp.float32),
    )
    matrix_parts = (
        lax.psum_scatter(
            mixer_grads[2].astype(jnp.bfloat16), "rep", scatter_dimension=1, tiled=True
        ).astype(jnp.float32),
        lax.psum_scatter(
            mixer_grads[5].astype(jnp.bfloat16), "rep", scatter_dimension=1, tiled=True
        ).astype(jnp.float32),
        lax.psum_scatter(
            dense_grads[2].astype(jnp.bfloat16), "rep", scatter_dimension=1, tiled=True
        ).astype(jnp.float32),
        lax.psum_scatter(
            dense_grads[4].astype(jnp.bfloat16), "rep", scatter_dimension=1, tiled=True
        ).astype(jnp.float32),
    )
    matrices = (
        lax.all_gather(matrix_parts[0].astype(jnp.bfloat16), "rep", axis=1, tiled=True).astype(
            jnp.float32
        ),
        lax.all_gather(matrix_parts[1].astype(jnp.bfloat16), "rep", axis=1, tiled=True).astype(
            jnp.float32
        ),
        lax.all_gather(matrix_parts[2].astype(jnp.bfloat16), "rep", axis=1, tiled=True).astype(
            jnp.float32
        ),
        lax.all_gather(matrix_parts[3].astype(jnp.bfloat16), "rep", axis=1, tiled=True).astype(
            jnp.float32
        ),
    )
    summed = lax.psum(
        (
            mixer_grads[0],
            mixer_grads[1],
            mixer_grads[3],
            mixer_grads[4],
            mixer_grads[6],
            dense_grads[0],
            dense_grads[1],
            dense_grads[3],
            dense_grads[5],
        ),
        "rep",
    )
    return (
        block_output.reshape(seqs, span, width),
        input_grad.reshape(seqs, span, width),
        summed[0],
        summed[1],
        matrices[0],
        summed[2],
        summed[3],
        matrices[1],
        summed[4],
        summed[5],
        summed[6],
        matrices[2],
        summed[7],
        matrices[3],
        summed[8],
    )


def solution(mesh):
    return jax.shard_map(
        local,
        mesh=mesh,
        in_specs=(
            P("rep", "shard", None),
            P("shard"),
            P("shard"),
            P("shard", None),
            P("shard"),
            P("shard"),
            P("shard", None),
            P("shard"),
            P("shard"),
            P("shard"),
            P("shard", None),
            P("shard"),
            P("shard", None),
            P("shard"),
            P("rep", "shard", None),
        ),
        out_specs=(
            P("rep", "shard", None),
            P("rep", "shard", None),
            P("shard"),
            P("shard"),
            P("shard", None),
            P("shard"),
            P("shard"),
            P("shard", None),
            P("shard"),
            P("shard"),
            P("shard"),
            P("shard", None),
            P("shard"),
            P("shard", None),
            P("shard"),
        ),
        check_vma=False,
    )
```

profile of v0, /device:TPU:0, one launch (start us, length us, event | category | flops | bytes accessed | tf_op | source)
XLA Modules:
  0.0 1219.9 jit_solution(8031042908517690960)
XLA Ops:
  17.6 14.3 %all-reduce.24 = (bf16[1088]{0:T(1024)(128)(2,1)S(1)}, bf16[1088]{0:T(1024)(128)(2,1)S(1)}, bf16[1088]{0:T(1024)(128)(2,1)S(1)}, bf16[1088]{0:T(1024)(128)(2,1)S...) all-reduce(bf16[1088]{0:T(1024)(128)(2,1)S(1)} %dynamic-update-slic, ...), channel_id=1, replica_groups=mesh['rep'=8,'shard'=4] {'shard'}, use_global_device_ids=true, to_apply=%add.1 | all-reduce | flops 11968 | bytes 47872
  32.4 32.4 %all-gather.14.cloned.1.call-done = bf16[1088,3264]{1,0:T(8,128)(2,1)} async-done(((bf16[272,3264]{1,0:T(8,128)(2,1)}), bf16[1088,3264]{1,0:T(8,128)(2,1)}) %all-gather.14.cloned.1.call-update) | async-done | bytes 7102480 | tf_op jit(solution)/shard_map/all_gather | solution.py:86
  64.7 6.7 fusion.87
  74.1 2.7 fusion.78
  79.7 18.2 %all-gather.24.cloned.1.call-done = bf16[1024,1088]{0,1:T(8,128)(2,1)} async-done(((bf16[256,1088]{0,1:T(8,128)(2,1)}), bf16[1024,1088]{0,1:T(8,128)(2,1)}) %all-gather.24.cloned.1.call-update) | async-done | bytes 2228240 | tf_op jit(solution)/shard_map/all_gather | solution.py:109
  97.9 5.2 copy.41
  103.2 20.5 %all-gather.26.cloned.1.call-done = bf16[1024,1088]{0,1:T(8,128)(2,1)} async-done(((bf16[256,1088]{0,1:T(8,128)(2,1)}), bf16[1024,1088]{0,1:T(8,128)(2,1)}) %all-gather.26.cloned.1.call-update) | async-done | bytes 2228240 | tf_op jit(solution)/shard_map/all_gather | solution.py:110
  123.7 5.2 copy.42
  129.0 51.8 %while.28 = (s32[]{:T(128)}, bf16[17,1,256,64]{2,3,1,0:T(8,128)(2,1)S(1)}, f32[17,1,256,1]{2,3,1,0:T(1,128)S(1)}, bf16[17,1,256,64]{3,2,1,0:T(8,128)(2,1)S(1)}, ...) while((s32[]{:T(128)}, ...), condition=%wide.region_5.6_spmd.clone, body=%wide.region_2.5_spmd.clone.sunk | while | flops 69205760 | bytes 3813473 | solution.py:131
  181.8 2.9 fusion.93
  185.0 31.1 %all-gather.18.cloned.1.call-done = bf16[1088,4352]{1,0:T(8,128)(2,1)} async-done(((bf16[272,4352]{1,0:T(8,128)(2,1)}), bf16[1088,4352]{1,0:T(8,128)(2,1)}) %all-gather.18.cloned.1.call-update) | async-done | bytes 9469968 | tf_op jit(solution)/shard_map/all_gather | solution.py:137
  216.0 16.9 %fusion.47 = (bf16[256,4352]{1,0:T(8,128)(2,1)}, f32[256,4352]{1,0:T(8,128)}) fusion(f32[4352]{0:T(1024)S(1)} %convert_element_type.247, bf16[1088,4352]{1,0:T(8,128)(2,1)} %all-gather.18.cloned.1.call-done, f32[256,1088]{0,1:T(8,128)S(1)} %get-tuple-element.251, f32[1088]{0:T(1024)S(1)} %convert_element_type.245, f32[1088]{0:T(1024)S(1)} %convert_element_type.244, ...), kind=kOutput, calls=%fused_computation.68 | convolution fusion | flops 2499231744 | bytes 17296896 | tf_op jit(solution)/shard_map/dot_general | solution.py:34
  232.9 52.1 %all-gather.20.cloned.1.call-done = bf16[4352,1088]{1,0:T(8,128)(2,1)} async-done(((bf16[1088,1088]{1,0:T(8,128)(2,1)}), bf16[4352,1088]{1,0:T(8,128)(2,1)}) %all-gather.20.cloned.1.call-update) | async-done | bytes 9469968 | tf_op jit(solution)/shard_map/all_gather | solution.py:139
  285.1 7.4 fusion.94
  292.9 3.0 multiply_reduce_fusion.1
  300.0 132.5 %while.29 = (s32[]{:T(128)}, bf16[17,1,256,64]{2,3,1,0:T(8,128)(2,1)S(1)}, bf16[17,1,1024,64]{2,3,1,0:T(8,128)(2,1)}, bf16[17,1,1024,64]{2,3,1,0:T(8,128)(2,1)},...) while((s32[]{:T(128)}, ...), condition=%wide.region_12.13_spmd.clone, body=%wide.region_10.12_spmd.clone.sunk | while | flops 170475264 | bytes 9514105 | solution.py:239
  312.1 1.8 fusion.148
  351.1 1.8 fusion.148
  360.6 1.8 fusion.149
  433.3 3.4 convolution_convert_fusion.3
  436.8 28.1 %reduce-scatter.15.cloned.1.call-done = bf16[1,256,1088]{1,2,0:T(8,128)(2,1)} async-done(((bf16[1,1024,1088]{1,2,0:T(8,128)(2,1)}), bf16[1,256,1088]{1,2,0:T(8,128)(2,1)}) %reduce-scatter.15.cloned.1.call-update) | async-done | bytes 557072 | tf_op jit(solution)/shard_map/reduce_scatter | solution.py:246
  464.9 35.0 %reduce-scatter.13.cloned.1.call-done = bf16[1,256,1088]{1,2,0:T(8,128)(2,1)} async-done(((bf16[1,1024,1088]{1,2,0:T(8,128)(2,1)}), bf16[1,256,1088]{1,2,0:T(8,128)(2,1)}) %reduce-scatter.13.cloned.1.call-update) | async-done | bytes 557072 | tf_op jit(solution)/shard_map/reduce_scatter | solution.py:243
  499.9 5.8 convolution_convert_fusion.2
  505.8 8.8 fusion.96
  514.7 7.5 convolution_convert_fusion.1
  522.3 14.8 %reduce-scatter.19.cloned.1.call-done = bf16[272,1088]{1,0:T(8,128)(2,1)} async-done(((bf16[1088,1088]{1,0:T(8,128)(2,1)}), bf16[272,1088]{1,0:T(8,128)(2,1)}) %reduce-scatter.19.cloned.1.call-update) | async-done | bytes 591888 | tf_op jit(solution)/shard_map/reduce_scatter | solution.py:277
  537.1 67.5 %reduce-scatter.17.cloned.1.call-done = bf16[272,3264]{1,0:T(8,128)(2,1)} async-done(((bf16[1088,3264]{1,0:T(8,128)(2,1)}), bf16[272,3264]{1,0:T(8,128)(2,1)}) %reduce-scatter.17.cloned.1.call-update) | async-done | bytes 1775632 | tf_op jit(solution)/shard_map/reduce_scatter | solution.py:268
  604.5 85.0 %reduce-scatter.23.cloned.1.call-done = bf16[1088,1088]{1,0:T(8,128)(2,1)} async-done(((bf16[4352,1088]{1,0:T(8,128)(2,1)}), bf16[1088,1088]{1,0:T(8,128)(2,1)}) %reduce-scatter.23.cloned.1.call-update) | async-done | bytes 2367504 | tf_op jit(solution)/shard_map/reduce_scatter | solution.py:181
  689.6 81.1 %reduce-scatter.21.cloned.1.call-done = bf16[272,4352]{1,0:T(8,128)(2,1)} async-done(((bf16[1088,4352]{1,0:T(8,128)(2,1)}), bf16[272,4352]{1,0:T(8,128)(2,1)}) %reduce-scatter.21.cloned.1.call-update) | async-done | bytes 2367504 | tf_op jit(solution)/shard_map/reduce_scatter | solution.py:175
  770.6 4.5 copy.54
  777.1 174.5 %all-reduce.27.cloned.1.call-done = (bf16[272,3264]{1,0:T(8,128)(2,1)}, bf16[272,1088]{1,0:T(8,128)(2,1)}, bf16[1088,1088]{1,0:T(8,128)(2,1)}) async-done(((bf16[272,3264]{1,0:T(8,128)(2,1)}, bf16[272,1088]{1,0:T(8,128)(2,1)}, bf16[1088,1088]{1,0:T(8,128)(2,1)}), (bf16[272,3264]{1,0:T(8,128)(2,1)}, bf16[272,1088]{1,0:T(8,128)(2,1)}, bf16[1088,1088]{1,0:T(8,128)(2,1)})) %all-reduce.27.cloned.1.call-update) | async-done | bytes 4734992
  951.5 1.8 dynamic-slice_bitcast_fusion
  953.4 78.3 %reduce-scatter.25.cloned.1.call-done = bf16[544,272]{1,0:T(8,128)(2,1)} async-done(((bf16[4352,272]{1,0:T(8,128)(2,1)}), bf16[544,272]{1,0:T(8,128)(2,1)}) %reduce-scatter.25.cloned.1.call-update) | async-done | bytes 295952
  1031.8 1.9 copy.55
  1037.6 2.2 constant_dynamic-slice_fusion.1
  1039.8 2.0 copy.47
  1041.8 6.5 fusion.76
  1048.4 11.4 all-reduce.23
  1060.5 36.5 %all-reduce.21 = (f32[272]{0:T(512)}, f32[272]{0:T(512)}, f32[272]{0:T(512)}, f32[272]{0:T(512)}, f32[272]{0:T(512)}, /*index=5*/f32[272]{0:T(512)}, f32[272]{0:T(512)}, f32[1088]{0:T(1024)}, f32[272]{0:T(512)}) all-reduce(f32[272]{0:T(512)S(1)} %dynamic-slice_convert_fusion.8, ...), channel_id=1, replica_groups=mesh['rep'=8,'shard'=4] {'rep'}, use_global_device_ids=true, to_apply=%region_19.20 | all-reduce | flops 3264 | bytes 26112 | tf_op jit(solution)/shard_map/psum | solution.py:312
  1097.0 2.7 fusion.75
  1099.7 8.9 fusion.61
  1109.8 34.2 %all_gather.81 = bf16[272,1088]{0,1:T(8,128)(2,1)S(1)} all-gather(bf16[272,136]{0,1:T(8,128)(2,1)S(1)} %copy.45), channel_id=1, replica_groups=mesh['rep'=8,'shard'=4] {'rep'}, dimensions={1}, use_global_device_ids=true | all-gather | bytes 665856 | tf_op jit(solution)/shard_map/all_gather | solution.py:302
  1145.3 5.0 copy.44
  1150.4 5.7 reshape.326
  1156.0 4.7 copy.46
  1160.7 7.1 reshape.327
  1167.8 40.2 %all-gather.22.cloned.1.call-done = bf16[1088,1088]{0,1:T(8,128)(2,1)} async-done(((bf16[1088,136]{0,1:T(8,128)(2,1)}), bf16[1088,1088]{0,1:T(8,128)(2,1)}) %all-gather.22.cloned.1.call-update) | async-done | bytes 2367504 | tf_op jit(solution)/shard_map/all_gather | solution.py:308
  1208.0 5.2 copy.49
  (327 shorter events, 206.1 us)
Async XLA Ops:
  7.2 24.8 %copy-start = (bf16[1,256,1088]{1,2,0:T(8,128)(2,1)S(1)}, bf16[1,256,1088]{1,2,0:T(8,128)(2,1)}, u32[]{:S(2)}) copy-start(bf16[1,256,1088]{1,2,0:T(8,128)(2,1)} %param.19) | copy-start | bytes 1671172
  7.2 57.6 %all-gather.14.cloned.1.call-start = ((), (), s32[]{:S(2)}) async-start(), calls=%async_computation.7 | async-start | bytes 9052160 | tf_op jit(solution)/shard_map/all_gather | solution.py:86
  7.9 90.0 %all-gather.24.cloned.1.call-start = ((), (), s32[]{:S(2)}) async-start(), calls=%async_computation.18 | async-start | bytes 2785280 | tf_op jit(solution)/shard_map/all_gather | solution.py:109
  71.4 1.7 copy-start.5
  74.1 49.7 %all-gather.26.cloned.1.call-start = ((), (), s32[]{:S(2)}) async-start(), calls=%async_computation.19 | async-start | bytes 2785280 | tf_op jit(solution)/shard_map/all_gather | solution.py:110
  76.9 104.0 %all-gather.16.cloned.1.call-start = ((), (), s32[]{:S(2)}) async-start(), calls=%async_computation.8 | async-start | bytes 3133440 | tf_op jit(solution)/shard_map/all_gather | solution.py:89
  77.5 138.6 %all-gather.18.cloned.1.call-start = ((), (), s32[]{:S(2)}) async-start(), calls=%async_computation.9 | async-start | bytes 11837440 | tf_op jit(solution)/shard_map/all_gather | solution.py:137
  78.1 207.0 %all-gather.20.cloned.1.call-start = ((), (), s32[]{:S(2)}) async-start(), calls=%async_computation.10 | async-start | bytes 12533760 | tf_op jit(solution)/shard_map/all_gather | solution.py:139
  78.6 386.3 %reduce-scatter.15.cloned.1.call-start = ((), (), s32[]{:S(2)}) async-start(), calls=%async_computation.12 | async-start | bytes 2785280 | tf_op jit(solution)/shard_map/reduce_scatter | solution.py:246
  180.8 1.0 copy-start.4
  180.8 3.9 copy-start.7
  185.0 100.1 %copy-start.1 = (f32[1,256,1088]{1,2,0:T(8,128)S(1)}, f32[1,256,1088]{1,2,0:T(8,128)}, u32[]{:S(2)}) copy-start(f32[1,256,1088]{1,2,0:T(8,128)} %param.33) | copy-start | bytes 3342340
  285.1 7.9 copy-start.9
  292.5 3.4 copy-start.6
  292.9 3.0 copy-start.2
  295.9 1.7 copy-start.10
  432.5 67.4 %reduce-scatter.13.cloned.1.call-start = ((), (), s32[]{:S(2)}) async-start(), calls=%async_computation.11 | async-start | bytes 2785280 | tf_op jit(solution)/shard_map/reduce_scatter | solution.py:243
  433.3 103.8 %reduce-scatter.19.cloned.1.call-start = ((), (), s32[]{:S(2)}) async-start(), calls=%async_computation.14 | async-start | bytes 3133440 | tf_op jit(solution)/shard_map/reduce_scatter | solution.py:277
  436.8 167.7 %reduce-scatter.17.cloned.1.call-start = ((), (), s32[]{:S(2)}) async-start(), calls=%async_computation.13 | async-start | bytes 9052160 | tf_op jit(solution)/shard_map/reduce_scatter | solution.py:268
  505.8 183.7 %reduce-scatter.23.cloned.1.call-start = ((), (), s32[]{:S(2)}) async-start(), calls=%async_computation.16 | async-start | bytes 12533760 | tf_op jit(solution)/shard_map/reduce_scatter | solution.py:181
  514.6 256.0 %reduce-scatter.21.cloned.1.call-start = ((), (), s32[]{:S(2)}) async-start(), calls=%async_computation.15 | async-start | bytes 11837440 | tf_op jit(solution)/shard_map/reduce_scatter | solution.py:175
  522.3 429.3 %all-reduce.27.cloned.1.call-start = ((), (), s32[]{:S(2)}) async-start(), calls=%async_computation.23 | async-start | bytes 9887744
  689.5 342.3 %reduce-scatter.25.cloned.1.call-start = ((), (), s32[]{:S(2)}) async-start(), calls=%async_computation.22 | async-start | bytes 3760128
  775.2 0.7 copy-start.11
  775.2 260.6 %copy-start.8 = (bf16[272]{0:T(512)(128)(2,1)S(1)}, bf16[272]{0:T(512)(128)(2,1)}, u32[]{:S(2)}) copy-start(bf16[272]{0:T(512)(128)(2,1)} %param.32) | copy-start | bytes 1636
  775.2 370.2 %all-gather.28.cloned.1.call-start = ((), (), s32[]{:S(2)}) async-start(), calls=%async_computation.20 | async-start | bytes 2506752 | tf_op jit(solution)/shard_map/all_gather | solution.py:299
  953.4 202.6 %all-gather.30.cloned.1.call-start = ((), (), s32[]{:S(2)}) async-start(), calls=%async_computation.21 | async-start | bytes 3133440 | tf_op jit(solution)/shard_map/all_gather | solution.py:305
  1033.7 174.3 %all-gather.22.cloned.1.call-start = ((), (), s32[]{:S(2)}) async-start(), calls=%async_computation.17 | async-start | bytes 2820096 | tf_op jit(solution)/shard_map/all_gather | solution.py:308
  1097.0 2.7 copy-start.3
Sparse Core Ops, SparseCore 0:
  9.6 55.1 all-gather.13
  74.2 23.7 all-gather.23
  100.1 23.5 all-gather.25
  125.1 24.9 all-gather.15
  151.5 64.4 all-gather.17
  217.4 67.5 all-gather.19
  432.6 32.2 reduce-scatter.14
  467.7 32.2 reduce-scatter.12
  503.1 33.9 reduce-scatter.18
  539.7 64.8 reduce-scatter.16
  607.1 82.3 reduce-scatter.22
  691.9 78.6 reduce-scatter.20
  774.6 176.8 all-reduce.26
  955.6 76.1 reduce-scatter.24
  1034.6 50.6 all-gather.27
  1088.1 64.4 all-gather.29
  1154.9 53.1 all-gather.21
where the time goes:
time: 1230 us; the launch traced here: 1220 us
  waiting for transfers between devices  762 us (62%)
  matrix products  254 us (21%)
  blocking collectives  96.5 us (8%)
  local copies, waits for them, and re-layouts  70.6 us (6%)
  between operations  18.4 us (1%)
  other arithmetic  17.1 us (1%)
    unnamed x19, waiting for transfers between devices  256 us
    reduce_scatter x1, waiting for transfers between devices, local(): lax.psum_scatter(down_weight_grad.astype(jnp.bfloat16), 'shard', scatter_...  85 us
    reduce_scatter x1, waiting for transfers between devices, local(): lax.psum_scatter(up_weight_grad.astype(jnp.bfloat16), 'shard', scatter_di...  81.1 us
    reduce_scatter x1, waiting for transfers between devices, local(): lax.psum_scatter(input_weight_grad.astype(jnp.bfloat16), 'shard', scatter...  67.5 us
    all_gather x1, waiting for transfers between devices, local(): lax.all_gather(down_weight, 'shard', axis=0, tiled=True)  52.1 us
    all_gather x1, waiting for transfers between devices, local(): lax.all_gather(matrix_parts[3].astype(jnp.bfloat16), 'rep', axis=1, tiled...  40.2 us
    psum x1, blocking collectives, local(): lax.psum((mixer_grads[0], mixer_grads[1], mixer_grads[3], mixer_grads[4],...  36.5 us
    dot_general x4, matrix products, matmul(): return jnp.dot(left, right, preferred_element_type=jnp.float32)  35.4 us
  transfers between devices with their start and end apart: 17, of which 14 were waited for; matrix products, arithmetic and copies ran while one was open for 15% of the time, Pallas kernels for 0%

commit v1 on v0

v1 whole, which is shorter than its diff:
```python
import functools

import jax
import jax.numpy as jnp
from jax import lax
from jax.experimental import pallas as pl
from jax.experimental.pallas import tpu as pltpu
from jax.sharding import PartitionSpec as P

HEADS = 17

epsilon = 1e-05
score_scale = 0.125
low = jnp.bfloat16
f32 = jnp.float32


def normalize(values):
    centre = jnp.mean(values, axis=-1, keepdims=True)
    centred = values - centre
    inverse = lax.rsqrt(jnp.mean(centred * centred, axis=-1, keepdims=True) + epsilon)
    return (centred * inverse, inverse)


def norm_back(grad, normed, inverse, gain):
    scaled = grad * gain
    first = jnp.mean(scaled, axis=-1, keepdims=True)
    second = jnp.mean(scaled * normed, axis=-1, keepdims=True)
    return inverse * (scaled - first - normed * second)


def gelu_parts(values):
    cumulative = 0.5 * (1.0 + lax.erf(values * 0.7071067811865476))
    density = jnp.exp(-0.5 * values * values) * 0.3989422804014327
    return values * cumulative, cumulative + values * density


def contract(left, right, left_dim, right_dim):
    return lax.dot_general(
        left, right, (((left_dim,), (right_dim,)), ((), ())), preferred_element_type=f32
    )


def swap(values, bit):
    size = lax.axis_size("shard")
    return lax.ppermute(values, "shard", [(i, i ^ bit) for i in range(size)])


def bits_far_first():
    bit = lax.axis_size("shard") // 2
    bits = []
    while bit:
        bits.append(bit)
        bit //= 2
    return bits


def relative_order():
    order = [0]
    for bit in bits_far_first():
        order = order + [o ^ bit for o in order]
    return order


def gather_relative(block):
    stack = block[None]
    for bit in bits_far_first():
        stack = jnp.concatenate([stack, swap(stack, bit)], axis=0)
    return stack


def gather_absolute(block):
    index = lax.axis_index("shard")
    stack = block[None]
    for bit in bits_far_first():
        other = swap(stack, bit)
        upper = (index & bit) != 0
        pair = jnp.stack(
            [jnp.where(upper, other, stack), jnp.where(upper, stack, other)], axis=1
        )
        stack = pair.reshape((2 * stack.shape[0],) + block.shape)
    return stack


def scatter_relative(parts):
    for bit in reversed(bits_far_first()):
        half = parts.shape[0] // 2
        other = swap(parts[half:].astype(low), bit)
        parts = parts[:half] + other.astype(f32)
    return parts[0]


def exchange(blocks):
    size = lax.axis_size("shard")
    index = lax.axis_index("shard")
    result = jnp.zeros_like(blocks)
    for offset in range(size):
        peer = index ^ offset
        piece = lax.dynamic_index_in_dim(blocks, peer, 0, keepdims=True)
        if offset:
            piece = swap(piece, offset)
        result = lax.dynamic_update_slice_in_dim(result, piece, peer, 0)
    return result


def visible_part(scores, top, block, fill):
    rows = lax.broadcasted_iota(jnp.int32, (block, block), 0)
    cols = lax.broadcasted_iota(jnp.int32, (block, block), 1)
    last = jnp.where(rows <= cols, scores[top:], fill)
    if top == 0:
        return last
    return jnp.concatenate([scores[:top], last], axis=0)


def turn(values):
    return values.astype(f32).T


def forward_kernel(blocks, block, place, q_ref, k_ref, v_ref, o_ref, low_ref, log_ref, k_rows, v_cols):
    for i in range(blocks):
        here = pl.ds(pl.multiple_of(place[i] * block, block), block)
        there = pl.ds(i * block, block)
        k_rows[there, :] = turn(k_ref[:, here]).astype(low)
        v_cols[:, there] = v_ref[:, here]
    for i in range(blocks):
        here = pl.ds(pl.multiple_of(place[i] * block, block), block)
        top = i * block
        count = top + block
        q_cols = q_ref[:, here] * jnp.asarray(score_scale, low)
        scores = contract(k_rows[:count, :], q_cols, 1, 0)
        scores = visible_part(scores, top, block, -jnp.inf)
        peak = jnp.max(scores, axis=0, keepdims=True)
        weights = jnp.exp(scores - peak)
        total = jnp.sum(weights, axis=0, keepdims=True)
        mixed = contract(v_cols[:, :count], weights.astype(low), 1, 0) / total
        o_ref[:, here] = mixed
        low_ref[:, here] = mixed.astype(low)
        log_ref[0, :, here] = peak + jnp.log(total)


def backward_kernel(
    blocks,
    block,
    place,
    q_ref,
    k_ref,
    v_ref,
    g_ref,
    o_ref,
    log_ref,
    dq_ref,
    dk_ref,
    dv_ref,
    k_rows,
    v_rows,
    k_cols,
    dk_rows,
    dv_rows,
):
    for i in range(blocks):
        here = pl.ds(pl.multiple_of(place[i] * block, block), block)
        there = pl.ds(i * block, block)
        k_rows[there, :] = turn(k_ref[:, here]).astype(low)
        v_rows[there, :] = turn(v_ref[:, here]).astype(low)
        k_cols[:, there] = k_ref[:, here]
    for i in reversed(range(blocks)):
        here = pl.ds(pl.multiple_of(place[i] * block, block), block)
        top = i * block
        count = top + block
        q_cols = q_ref[:, here] * jnp.asarray(score_scale, low)
        g_cols = g_ref[:, here]
        q_rows = turn(q_cols).astype(low)
        g_rows = turn(g_cols).astype(low)
        correction = jnp.sum(g_cols.astype(f32) * o_ref[:, here], axis=0, keepdims=True)
        scores = contract(k_rows[:count, :], q_cols, 1, 0)
        probs = jnp.exp(scores - log_ref[0, :, here])
        probs = visible_part(probs, top, block, 0.0)
        grad_probs = contract(v_rows[:count, :], g_cols, 1, 0)
        grad_scores = (probs * (grad_probs - correction)).astype(low)
        dv_part = contract(probs.astype(low), g_rows, 1, 0)
        dk_part = contract(grad_scores, q_rows, 1, 0)
        if i == blocks - 1:
            dv_rows[:count, :] = dv_part
            dk_rows[:count, :] = dk_part
        else:
            dv_rows[:count, :] += dv_part
            dk_rows[:count, :] += dk_part
        dq = contract(k_cols[:, :count], grad_scores, 1, 0) * score_scale
        dq_ref[:, here] = dq.astype(low)
    for i in range(blocks):
        here = pl.ds(pl.multiple_of(place[i] * block, block), block)
        there = pl.ds(i * block, block)
        dk_ref[:, here] = dk_rows[there, :].T.astype(low)
        dv_ref[:, here] = dv_rows[there, :].T.astype(low)


def head_spec(size, length, first):
    return pl.BlockSpec((size, length), lambda h, place: (first + h, 0))


def attend_forward(place, projected, heads, block):
    size = projected.shape[0] // (3 * heads)
    length = projected.shape[1]
    blocks = length // block
    row = pl.BlockSpec((1, 1, length), lambda h, place: (h, 0, 0))
    return pl.pallas_call(
        functools.partial(forward_kernel, blocks, block),
        grid_spec=pltpu.PrefetchScalarGridSpec(
            num_scalar_prefetch=1,
            grid=(heads,),
            in_specs=[
                head_spec(size, length, 0),
                head_spec(size, length, heads),
                head_spec(size, length, 2 * heads),
            ],
            out_specs=[head_spec(size, length, 0), head_spec(size, length, 0), row],
            scratch_shapes=[
                pltpu.VMEM((length, size), low),
                pltpu.VMEM((size, length), low),
            ],
        ),
        out_shape=[
            jax.ShapeDtypeStruct((heads * size, length), f32),
            jax.ShapeDtypeStruct((heads * size, length), low),
            jax.ShapeDtypeStruct((heads, 1, length), f32),
        ],
        cost_estimate=pl.CostEstimate(
            flops=4 * heads * length * length * size,
            bytes_accessed=heads * length * size * 12,
            transcendentals=heads * length * length,
        ),
        compiler_params=pltpu.CompilerParams(vmem_limit_bytes=32 * 1024 * 1024),
        name="attend_forward",
    )(place, projected, projected, projected)


def attend_backward(place, projected, grad, mixed, log_total, heads, block):
    size = projected.shape[0] // (3 * heads)
    length = projected.shape[1]
    blocks = length // block
    row = pl.BlockSpec((1, 1, length), lambda h, place: (h, 0, 0))
    out = jax.ShapeDtypeStruct((heads * size, length), low)
    return pl.pallas_call(
        functools.partial(backward_kernel, blocks, block),
        grid_spec=pltpu.PrefetchScalarGridSpec(
            num_scalar_prefetch=1,
            grid=(heads,),
            in_specs=[
                head_spec(size, length, 0),
                head_spec(size, length, heads),
                head_spec(size, length, 2 * heads),
                head_spec(size, length, 0),
                head_spec(size, length, 0),
                row,
            ],
            out_specs=[head_spec(size, length, 0)] * 3,
            scratch_shapes=[
                pltpu.VMEM((length, size), low),
                pltpu.VMEM((length, size), low),
                pltpu.VMEM((size, length), low),
                pltpu.VMEM((length, size), f32),
                pltpu.VMEM((length, size), f32),
            ],
        ),
        out_shape=[out, out, out],
        cost_estimate=pl.CostEstimate(
            flops=10 * heads * length * length * size,
            bytes_accessed=heads * length * size * 20,
            transcendentals=heads * length * length,
        ),
        compiler_params=pltpu.CompilerParams(vmem_limit_bytes=32 * 1024 * 1024),
        name="attend_backward",
    )(place, projected, projected, projected, grad, mixed, log_total)


def local(
    block_input,
    first_gain,
    first_shift,
    query_key_value_weight,
    query_bias,
    value_bias,
    attention_output_weight,
    attention_output_bias,
    second_gain,
    second_shift,
    up_weight,
    up_bias,
    down_weight,
    down_bias,
    cotangent,
):
    shards = lax.axis_size("shard")
    index = lax.axis_index("shard")
    seqs, span, width = block_input.shape
    size = width // HEADS
    own = width // shards
    hidden = up_bias.shape[0]
    starts = [d * own // size for d in range(shards)]
    heads = max(-(-(d + 1) * own // size) - starts[d] for d in range(shards))
    window = heads * size
    pad = window - own
    start = index * own // size
    skew = index * own - start * size
    order = relative_order()
    inverse_order = jnp.asarray([order.index(o) for o in range(shards)], jnp.int32)
    place = inverse_order[jnp.arange(shards, dtype=jnp.int32) ^ index]

    own_input = block_input.reshape(seqs * span, width)
    inputs_all = gather_relative(own_input)
    vectors = gather_absolute(
        jnp.stack(
            [
                first_gain,
                first_shift,
                query_bias,
                value_bias,
                attention_output_bias,
                second_gain,
                second_shift,
                down_bias,
            ]
        )
    )
    vectors = vectors.transpose(1, 0, 2).reshape(8, width)
    gain_one, shift_one, bias_query, bias_value, bias_out, gain_two, shift_two, bias_down = (
        vectors[i] for i in range(8)
    )
    weight_in = exchange(
        jnp.stack(
            [
                jnp.concatenate(
                    [
                        query_key_value_weight[
                            :, part * width + s * size : part * width + s * size + window
                        ]
                        for part in range(3)
                    ],
                    axis=1,
                )
                for s in starts
            ]
        )
    ).reshape(width, 3 * window)
    weight_up = exchange(
        up_weight.reshape(own, shards, hidden).transpose(1, 0, 2)
    ).reshape(width, hidden)
    to_right = [(i, i + 1) for i in range(shards - 1)]
    to_left = [(i + 1, i) for i in range(shards - 1)]
    weight_out_window = lax.dynamic_slice_in_dim(
        jnp.concatenate(
            [
                lax.ppermute(attention_output_weight[own - pad :], "shard", to_right),
                attention_output_weight,
                lax.ppermute(attention_output_weight[:pad], "shard", to_left),
            ],
            axis=0,
        ),
        pad - skew,
        window,
        0,
    )
    branch_all = gather_relative(cotangent.reshape(seqs * span, width).astype(low))
    grad_out = cotangent.reshape(seqs * span, width)

    def own_rows(values):
        return lax.dynamic_slice_in_dim(values, skew, own, 0)

    rows = shards * seqs * span
    normed_all, _ = normalize(inputs_all.reshape(rows, width).astype(f32))
    hidden_one = (normed_all * gain_one + shift_one).astype(low)
    bias_window = jnp.concatenate(
        [
            lax.dynamic_slice_in_dim(bias_query, start * size, window, 0),
            jnp.zeros((window,), low),
            lax.dynamic_slice_in_dim(bias_value, start * size, window, 0),
        ]
    ).astype(f32)
    projected = (contract(weight_in, hidden_one, 0, 1) + bias_window[:, None]).astype(low)

    def per_sequence(values):
        lead = values.shape[:-1]
        split = values.reshape(lead + (shards, seqs, span))
        return [split[..., :, s, :].reshape(lead + (shards * span,)) for s in range(seqs)]

    def join_sequences(parts):
        if seqs == 1:
            return parts[0]
        lead = parts[0].shape[:-1]
        joined = jnp.stack([p.reshape(lead + (shards, span)) for p in parts], axis=-2)
        return joined.reshape(lead + (rows,))

    projected_parts = per_sequence(projected) if seqs > 1 else [projected]
    forward_parts = [attend_forward(place, p, heads, span) for p in projected_parts]
    attended = own_rows(join_sequences([p[1] for p in forward_parts]))
    mixed_sum = scatter_relative(
        contract(attended, attention_output_weight, 0, 0).reshape(shards, seqs * span, width)
    )
    layer_input = own_input.astype(f32)
    middle = layer_input + mixed_sum + bias_out

    normed_two, inverse_two = normalize(middle)
    hidden_two = gather_relative((normed_two * gain_two + shift_two).astype(low)).reshape(
        rows, width
    )
    branch = branch_all.reshape(rows, width)
    before = contract(hidden_two, weight_up, 1, 0) + up_bias
    activated, slope = gelu_parts(before)
    activated = activated.astype(low)
    grad_before = (contract(branch, down_weight, 1, 1) * slope).astype(low)
    grad_hidden_two = scatter_relative(
        contract(grad_before, weight_up, 1, 1).reshape(shards, seqs * span, width)
    )
    down_weight_grad = lax.psum(contract(activated, branch, 0, 0).astype(low), "rep")
    up_weight_grad = exchange(
        contract(hidden_two, grad_before, 0, 0).astype(low).reshape(shards, own, hidden)
    )
    up_weight_grad = lax.psum(up_weight_grad, "rep")
    block_output = (
        middle
        + scatter_relative(
            contract(activated, down_weight, 1, 0).reshape(shards, seqs * span, width)
        )
        + bias_down
    )
    grad_middle = grad_out + norm_back(grad_hidden_two, normed_two, inverse_two, gain_two)

    grad_mixed = gather_relative(grad_middle.astype(low)).reshape(rows, width)
    grad_attended = contract(weight_out_window, grad_mixed, 1, 1).astype(low)
    grad_parts = per_sequence(grad_attended) if seqs > 1 else [grad_attended]
    backward_parts = [
        attend_backward(place, p, g, f[0], f[2], heads, span)
        for p, g, f in zip(projected_parts, grad_parts, forward_parts)
    ]
    grad_query, grad_key, grad_value = (
        join_sequences([p[i] for p in backward_parts]) for i in range(3)
    )
    own_query, own_key, own_value = (own_rows(g) for g in (grad_query, grad_key, grad_value))
    own_projected = jnp.concatenate([own_query, own_key, own_value], axis=0)
    line = jnp.arange(window)
    mine = ((line >= skew) & (line < skew + own))[:, None]
    grad_projected = jnp.concatenate(
        [jnp.where(mine, g, jnp.zeros_like(g)) for g in (grad_query, grad_key, grad_value)], axis=0
    )
    input_weight_grad = exchange(
        contract(hidden_one, own_projected, 0, 1).astype(low).reshape(shards, own, 3 * own)
    )
    input_weight_grad = lax.psum(input_weight_grad, "rep")
    output_weight_grad = lax.psum(contract(attended, grad_mixed, 1, 0).astype(low), "rep")
    grad_hidden_one = scatter_relative(
        contract(grad_projected, weight_in, 0, 1).reshape(shards, seqs * span, width)
    )
    normed_one, inverse_one = normalize(layer_input)
    input_grad = grad_middle + norm_back(grad_hidden_one, normed_one, inverse_one, gain_one)

    def own_part(values):
        return lax.dynamic_slice_in_dim(values, index * own, own, 0)

    partial = lax.psum(
        jnp.stack(
            [
                jnp.sum(grad_hidden_one * normed_one, axis=0),
                jnp.sum(grad_hidden_one, axis=0),
                jnp.sum(grad_hidden_two * normed_two, axis=0),
                jnp.sum(grad_hidden_two, axis=0),
            ]
        ),
        ("rep", "shard"),
    )
    first_gain_grad, first_shift_grad, second_gain_grad, second_shift_grad = (
        own_part(partial[i]) for i in range(4)
    )
    complete = lax.psum(
        jnp.concatenate(
            [
                jnp.sum(own_query.astype(f32), axis=1),
                jnp.sum(own_value.astype(f32), axis=1),
                own_part(jnp.sum(grad_mixed.astype(f32), axis=0)),
                own_part(jnp.sum(branch.astype(f32), axis=0)),
                jnp.sum(grad_before.astype(f32), axis=0),
            ]
        ),
        "rep",
    )
    query_bias_grad, value_bias_grad, output_bias_grad, down_bias_grad = (
        complete[i * own : (i + 1) * own] for i in range(4)
    )
    up_bias_grad = complete[4 * own :]
    return (
        block_output.reshape(seqs, span, width),
        input_grad.reshape(seqs, span, width),
        first_gain_grad,
        first_shift_grad,
        input_weight_grad.reshape(shards, own, 3, own)
        .transpose(1, 2, 0, 3)
        .reshape(own, 3 * width)
        .astype(f32),
        query_bias_grad,
        value_bias_grad,
        output_weight_grad.astype(f32),
        output_bias_grad,
        second_gain_grad,
        second_shift_grad,
        up_weight_grad.transpose(1, 0, 2).reshape(own, shards * hidden).astype(f32),
        up_bias_grad,
        down_weight_grad.astype(f32),
        down_bias_grad,
    )


def solution(mesh):
    matrix, vector, tokens = P("shard", None), P("shard"), P("rep", "shard", None)
    return jax.shard_map(
        local,
        mesh=mesh,
        in_specs=(
            tokens,
            vector,
            vector,
            matrix,
            vector,
            vector,
            matrix,
            vector,
            vector,
            vector,
            matrix,
            vector,
            matrix,
            vector,
            tokens,
        ),
        out_specs=(
            tokens,
            tokens,
            vector,
            vector,
            matrix,
            vector,
            vector,
            matrix,
            vector,
            vector,
            vector,
            matrix,
            vector,
            matrix,
            vector,
        ),
        check_vma=False,
    )
```

time: 1230 us -> 619 us (0.50)
  waiting for transfers between devices: 762 us -> 251 us
  matrix products: 254 us -> 44.3 us
  local copies, waits for them, and re-layouts: 70.6 us -> 119 us
  other arithmetic: 17.1 us -> 54.8 us
  starting transfers between devices: 0.86 us -> 27.9 us
  Pallas kernels: 0 us -> 20.8 us
  blocking collectives: 96.5 us -> 80.5 us
    reduce_scatter x6 -> x0, waiting for transfers between devices: 311 us -> none  [the longest x1 85 us: local(): lax.psum_scatter(down_weight_grad.astype(jnp.bfloat16), 'shard', scatter_...]
    unnamed x19 -> x1, waiting for transfers between devices: 256 us -> 0.02 us
    dot_general x131 -> x12, matrix products: 254 us -> 44.3 us  [contract(): lax.dot_general(left, right, (((left_dim,), (right_dim,)), ((), ())), pre...]
    all_gather x9 -> x0, waiting for transfers between devices: 195 us -> none  [the longest x1 52.1 us: local(): lax.all_gather(down_weight, 'shard', axis=0, tiled=True)]
    psum x0 -> x1, waiting for transfers between devices: none -> 148 us  [local(): input_weight_grad = lax.psum(input_weight_grad, 'rep')]
    ppermute x0 -> x32, waiting for transfers between devices: none -> 104 us  [the longest x30 104 us: swap(): return lax.ppermute(values, 'shard', [(i, i ^ bit) for i in range(size)])]
    psum x1 -> x2, blocking collectives: 36.5 us -> 80.5 us  [the longest x1 40.6 us: local(): lax.psum(jnp.stack([jnp.sum(grad_hidden_one * normed_one, axis=0), jnp.su...]
    all_gather x1 -> x0, blocking collectives: 34.2 us -> none  [local(): lax.all_gather(matrix_parts[1].astype(jnp.bfloat16), 'rep', axis=1, tiled...]
  transfers between devices with their start and end apart: 17 -> 33, of which waited for: 14 -> 12; matrix products, arithmetic and copies ran while one was open for 15% -> 26% of each run, Pallas kernels for 0% -> 2%
where the time goes in v1:
time: 619 us; the launch traced here: 614 us
  waiting for transfers between devices  251 us (41%)
  local copies, waits for them, and re-layouts  119 us (19%)
  blocking collectives  80.5 us (13%)
  other arithmetic  54.8 us (9%)
  matrix products  44.3 us (7%)
  starting transfers between devices  27.9 us (5%)
  Pallas kernels  20.8 us (3%)
  between operations  15.2 us (2%)
    psum x1, waiting for transfers between devices, local(): input_weight_grad = lax.psum(input_weight_grad, 'rep')  148 us
    ppermute x30, waiting for transfers between devices, swap(): return lax.ppermute(values, 'shard', [(i, i ^ bit) for i in range(size)])  104 us
    dot_general x12, matrix products, contract(): lax.dot_general(left, right, (((left_dim,), (right_dim,)), ((), ())), pre...  44.3 us
    psum x1, blocking collectives, local(): lax.psum(jnp.stack([jnp.sum(grad_hidden_one * normed_one, axis=0), jnp.su...  40.6 us
    psum x1, blocking collectives, local(): lax.psum(jnp.concatenate([jnp.sum(own_query.astype(f32), axis=1), jnp.sum...  39.9 us
    ppermute x30, starting transfers between devices, swap(): return lax.ppermute(values, 'shard', [(i, i ^ bit) for i in range(size)])  24.6 us
    dynamic_update_slice x14, local copies, waits for them, and re-layouts, exchange(): result = lax.dynamic_update_slice_in_dim(result, piece, peer, 0)  17.7 us
  transfers between devices with their start and end apart: 33, of which 12 were waited for; matrix products, arithmetic and copies ran while one was open for 26% of the time, Pallas kernels for 2%

profile of v1, /device:TPU:0, one launch (start us, length us, event | category | flops | bytes accessed | tf_op | source)
XLA Modules:
  0.0 613.9 jit_solution(11194128015810706108)
XLA Ops:
  13.5 2.9 collective-permute-start.5
  16.4 3.2 fusion.75
  28.1 4.2 collective-permute-done.3
  34.5 6.8 %reshape.546 = bf16[272,4,1088]{2,1,0:T(4,128)(2,1)} reshape(bf16[272,4352]{1,0:T(8,128)(2,1)} %param.26) | data formatting | bytes 4734976 | tf_op jit(solution)/shard_map/reshape | solution.py:346
  46.6 6.6 %collective-permute-done.2 = bf16[1,272,960]{2,1,0:T(8,128)(2,1)} collective-permute-done((bf16[1,272,960]{2,1,0:T(8,128)(2,1)}, bf16[1,272,960]{2,1,0:T(8,128)(2,1)}, u32[]{:S(2)}, u32[]{:S(2)}) %collective-permute-start.2) | collective-permute-done | bytes 522272 | tf_op jit(solution)/shard_map/ppermute | solution.py:46
  59.0 3.1 add_convert_fusion
  62.1 4.2 copy.67
  66.3 5.3 add_convert_fusion.1.q_ref.k_ref.v_ref
  71.6 10.2 %attend_forward.1 = (f32[320,1024]{1,0:T(8,128)S(1)}, bf16[320,1024]{1,0:T(8,128)(2,1)S(1)}, f32[5,1,1024]{2,1,0:T(1,128)S(1)}) custom-call(s32[4]{0:T(128)S(1)} %gather_fusion, bf16[960,1024]{1,0:T(8,128)(2,1)S(1)} %add_convert_fusion.1.q_ref.k_ref.v_ref, bf16[960,1024]{1,0:T(8,128)(2,1)S(1)} %add_convert_fusion.1.q_ref.k_ref.v_ref, ...), custom_call_target="tpu_custom_call" | custom-call | flops 1342177280 | bytes 3932160 | tf_op jit(solution)/shard_map/attend_forward/pallas_call | solution.py:206
  85.0 5.4 constant_dynamic-slice_fusion.13
  102.0 34.2 %collective-permute-done.16 = bf16[1,256,1088]{1,2,0:T(8,128)(2,1)} collective-permute-done((bf16[1,256,1088]{1,2,0:T(8,128)(2,1)}, bf16[1,256,1088]{1,2,0:T(8,128)(2,1)}, u32[]{:S(2)}, u32[]{:S(2)}) %collective-permute-start.16) | collective-permute-done | bytes 557088 | tf_op jit(solution)/shard_map/ppermute | solution.py:46
  138.4 8.7 %collective-permute-done.8 = bf16[1,256,1088]{1,2,0:T(8,128)(2,1)} collective-permute-done((bf16[1,256,1088]{1,2,0:T(8,128)(2,1)}, bf16[1,256,1088]{1,2,0:T(8,128)(2,1)}, u32[]{:S(2)}, u32[]{:S(2)}) %collective-permute-start.8) | collective-permute-done | bytes 557088 | tf_op jit(solution)/shard_map/ppermute | solution.py:46
  150.1 2.8 add_convert_fusion.2
  158.2 8.6 %collective-permute-done.9 = bf16[1,256,1088]{1,2,0:T(8,128)(2,1)} collective-permute-done((bf16[1,256,1088]{1,2,0:T(8,128)(2,1)}, bf16[1,256,1088]{1,2,0:T(8,128)(2,1)}, u32[]{:S(2)}, u32[]{:S(2)}) %collective-permute-start.9) | collective-permute-done | bytes 557088 | tf_op jit(solution)/shard_map/ppermute | solution.py:46
  175.5 3.2 convert_reduce_fusion.1
  178.7 4.2 copy.77
  183.0 4.0 fusion.70
  186.9 5.8 copy.83
  192.7 3.1 pad_maximum_fusion.2
  195.9 4.2 copy.70
  200.1 6.4 %multiply_convert_fusion = (bf16[1024,1088]{0,1:T(8,128)(2,1)S(1)}, f32[1024,1088]{0,1:T(8,128)S(1)}) fusion(f32[1088]{0:T(1024)S(1)} %convert_element_type.258, bf16[1024,1088]{1,0:T(8,128)(2,1)} %bitcast.179, bf16[1088,1088]{1,0:T(8,128)(2,1)} %bitcast.175), kind=kOutput, calls=%fused_computation.18 | convolution fusion | flops 2430992384 | bytes 11284736 | tf_op jit(solution)/shard_map/dot_general | solution.py:39
  206.5 5.0 convert_reduce_fusion
  211.6 3.1 fusion.80
  215.0 3.2 fusion.79
  227.2 11.7 %collective-permute-done.19 = bf16[1,256,1088]{1,2,0:T(8,128)(2,1)S(1)} collective-permute-done((bf16[1,256,1088]{1,2,0:T(8,128)(2,1)S(1)}, bf16[1,256,1088]{1,2,0:T(8,128)(2,1)S(1)}, u32[]{:S(2)}, u32[]{:S(2)}) %collective-permute-start.19) | collective-permute-done | bytes 557088 | tf_op jit(solution)/shard_map/ppermute | solution.py:46
  239.6 11.0 %collective-permute-done.15 = bf16[1,256,1088]{1,2,0:T(8,128)(2,1)S(1)} collective-permute-done((bf16[1,256,1088]{1,2,0:T(8,128)(2,1)S(1)}, bf16[1,256,1088]{1,2,0:T(8,128)(2,1)S(1)}, u32[]{:S(2)}, u32[]{:S(2)}) %collective-permute-start.15) | collective-permute-done | bytes 557088 | tf_op jit(solution)/shard_map/ppermute | solution.py:46
  254.3 3.3 convolution_convert_fusion.1
  259.6 8.5 %collective-permute-done.22 = bf16[1,256,1088]{1,2,0:T(8,128)(2,1)S(1)} collective-permute-done((bf16[1,256,1088]{1,2,0:T(8,128)(2,1)S(1)}, bf16[1,256,1088]{1,2,0:T(8,128)(2,1)S(1)}, u32[]{:S(2)}, u32[]{:S(2)}) %collective-permute-start.22) | collective-permute-done | bytes 557088 | tf_op jit(solution)/shard_map/ppermute | solution.py:46
  268.3 4.3 convolution_convert_fusion
  274.5 7.0 %collective-permute-done.30 = bf16[1,272,1088]{2,1,0:T(8,128)(2,1)S(1)} collective-permute-done((bf16[1,272,1088]{2,1,0:T(8,128)(2,1)S(1)}, bf16[1,272,1088]{2,1,0:T(8,128)(2,1)S(1)}, u32[]{:S(2)}, u32[]{:S(2)}) %collective-permute-start.30) | collective-permute-done | bytes 591904 | tf_op jit(solution)/shard_map/ppermute | solution.py:46
  283.8 3.0 copy.80
  286.8 2.9 convolution_convert_fusion.4.g_ref
  289.8 10.6 %attend_backward.1 = (bf16[320,1024]{1,0:T(8,128)(2,1)S(1)}, bf16[320,1024]{1,0:T(8,128)(2,1)S(1)}, bf16[320,1024]{1,0:T(8,128)(2,1)S(1)}) custom-call(s32[4]{0:T(128)S(1)} %gather_fusion, bf16[960,1024]{1,0:T(8,128)(2,1)S(1)} %copy-done.3, bf16[960,1024]{1,0:T(8,128)(2,1)S(1)} %copy-done.3, bf16[960,1024]{1,0:T(8,128)(2,1)S(1)} %copy-done.3, ...), custom_call_target="tpu_custom_call" | custom-call | flops 3355443200 | bytes 6553600 | tf_op jit(solution)/shard_map/attend_backward/pallas_call | solution.py:243
  302.0 3.6 convolution_convert_fusion.2
  305.6 4.0 copy.84
  309.6 2.8 constant_dynamic-slice_fusion.4
  315.4 2.4 copy.90
  317.8 5.5 convert_element_type.292
  323.5 3.4 convolution_convert_fusion.3
  339.1 6.8 %copy.89 = bf16[272,3,4,272]{3,2,1,0:T(4,128)(2,1)} copy(bf16[272,3,4,272]{0,3,1,2:T(8,128)(2,1)} %bitcast.32) | data formatting | bytes 3551232 | tf_op jit(solution)/shard_map/convert_element_type | solution.py:497
  345.9 4.7 convert_element_type.281
  352.2 2.5 fusion.9
  361.1 39.9 %psum.44 = f32[2176]{0:T(1024)S(1)} all-reduce(f32[2176]{0:T(1024)S(1)} %concatenate.75), channel_id=1, replica_groups=mesh['rep'=8,'shard'=4] {'rep'}, use_global_device_ids=true, to_apply=%region_21.22 | all-reduce | flops 2176 | bytes 17408 | tf_op jit(solution)/shard_map/psum | solution.py:473
  405.8 40.6 %psum.42 = f32[4,1088]{1,0:T(4,128)S(1)} all-reduce(f32[4,1088]{1,0:T(4,128)S(1)} %pad_maximum_fusion.10), channel_id=1, replica_groups=mesh['rep'=8,'shard'=4] {'rep','shard'}, use_global_device_ids=true, to_apply=%region_14.15 | all-reduce | flops 4352 | bytes 34816 | tf_op jit(solution)/shard_map/psum | solution.py:459
  449.1 147.5 %all-reduce.3.cloned.1.call-done = (bf16[272,3264]{1,0:T(8,128)(2,1)}, bf16[272,1088]{1,0:T(8,128)(2,1)}, bf16[272,4352]{1,0:T(8,128)(2,1)}, bf16[1088,1088]{1,0:T(8,128)(2,1)}) async-done(((bf16[272,3264]{1,0:T(8,128)(2,1)}, bf16[272,1088]{1,0:T(8,128)(2,1)}, bf16[272,4352]{1,0:T(8,128)(2,1)}, bf16[1088,1088]{1,0:T(8,128)(2,1)}), (bf16[272,3264]{1,0:T(8,128)(2,1)}, bf16[272,1088]{1,0:T(8,128)(2,1)}, ...) | async-done | bytes 7102480 | tf_op jit(solution)/shard_map/psum | solution.py:448
  596.6 3.7 convert_element_type.282
  601.4 2.5 convert_element_type.293
  604.2 2.6 convert_element_type.295
  (275 shorter events, 115.4 us)
Async XLA Ops:
  7.2 199.3 %copy-start = (bf16[1088,1088]{1,0:T(8,128)(2,1)S(1)}, bf16[1088,1088]{1,0:T(8,128)(2,1)}, u32[]{:S(2)}) copy-start(bf16[1088,1088]{1,0:T(8,128)(2,1)} %param.28) | copy-start | bytes 7102468
  7.2 589.4 %all-reduce.3.cloned.1.call-start = ((), (), s32[]{:S(2)}) async-start(), calls=%async_computation | async-start | bytes 14622720 | tf_op jit(solution)/shard_map/psum | solution.py:448
  13.5 13.7 %collective-permute-start.5 = (bf16[1,8,272]{2,1,0:T(8,128)(2,1)}, bf16[1,8,272]{2,1,0:T(8,128)(2,1)}, u32[]{:S(2)}, u32[]{:S(2)}) collective-permute-start(bf16[1,8,272]{2,1,0:T(8,128)(2,1)} %bitcast.6), channel_id=1, source_target_pairs={{0,2},{1,3},{2,0},{3,1},{4,6},{5,7},{6,4},{7,5},{8,10},{9,11},{10,... | collective-permute-start | bytes 13064 | tf_op jit(solution)/shard_map/ppermute | solution.py:46
  16.4 15.9 %collective-permute-start.3 = (bf16[1,256,1088]{1,2,0:T(8,128)(2,1)}, bf16[1,256,1088]{1,2,0:T(8,128)(2,1)}, u32[]{:S(2)}, u32[]{:S(2)}) collective-permute-start(bf16[1,256,1088]{1,2,0:T(8,128)(2,1)} %param.16), channel_id=1, source_target_pairs={{0,2},{1,3},{2,0},{3,1},{4,6},{5,7},{6,4},{7,5},{8,10},{9,11},{10,... | collective-permute-start | bytes 1671176 | tf_op jit(solution)/shard_map/ppermute | solution.py:46
  22.4 9.9 %copy-start.7 = (bf16[1,256,1088]{1,2,0:T(8,128)(2,1)S(1)}, bf16[1,256,1088]{1,2,0:T(8,128)(2,1)}, u32[]{:S(2)}) copy-start(bf16[1,256,1088]{1,2,0:T(8,128)(2,1)} %param.16) | copy-start | bytes 1671172
  25.0 17.7 %collective-permute-start = (bf16[1,272,960]{2,1,0:T(8,128)(2,1)}, bf16[1,272,960]{2,1,0:T(8,128)(2,1)}, u32[]{:S(2)}, u32[]{:S(2)}) collective-permute-start(bf16[1,272,960]{2,1,0:T(8,128)(2,1)} %get-tuple-element.72), channel_id=1, source_target_pairs={{0,1},{1,0},{2,3},{3,2},{4,5},{5,4},{6,7},{7,6},{8,9},{9,8},{10,11... | collective-permute-start | bytes 1566728 | tf_op jit(solution)/shard_map/ppermute | solution.py:46
  25.0 19.6 %collective-permute-start.1 = (bf16[1,272,960]{2,1,0:T(8,128)(2,1)}, bf16[1,272,960]{2,1,0:T(8,128)(2,1)}, u32[]{:S(2)}, u32[]{:S(2)}) collective-permute-start(bf16[1,272,960]{2,1,0:T(8,128)(2,1)} %get-tuple-element.71), channel_id=1, source_target_pairs={{0,2},{1,3},{2,0},{3,1},{4,6},{5,7},{6,4},{7,5},{8,10},{9,11},{10,... | collective-permute-start | bytes 1566728 | tf_op jit(solution)/shard_map/ppermute | solution.py:46
  27.0 26.2 %collective-permute-start.2 = (bf16[1,272,960]{2,1,0:T(8,128)(2,1)}, bf16[1,272,960]{2,1,0:T(8,128)(2,1)}, u32[]{:S(2)}, u32[]{:S(2)}) collective-permute-start(bf16[1,272,960]{2,1,0:T(8,128)(2,1)} %get-tuple-element.70), channel_id=1, source_target_pairs={{0,3},{1,2},{2,1},{3,0},{4,7},{5,6},{6,5},{7,4},{8,11},{9,10},{10,... | collective-permute-start | bytes 1566728 | tf_op jit(solution)/shard_map/ppermute | solution.py:46
  27.9 14.0 %collective-permute-start.6 = (bf16[2,8,272]{2,1,0:T(8,128)(2,1)S(1)}, bf16[2,8,272]{2,1,0:T(8,128)(2,1)S(1)}, u32[]{:S(2)}, u32[]{:S(2)}) collective-permute-start(bf16[2,8,272]{2,1,0:T(8,128)(2,1)S(1)} %maximum_bitcast_fusion.4), channel_id=1, source_target_pairs={{0,1},{1,0},{2,3},{3,2},{4,5},{5,4},{6,7},{7,6},{8,9},{9,8},{10,11... | collective-permute-start | bytes 26120 | tf_op jit(solution)/shard_map/ppermute | solution.py:46
  34.4 20.7 %collective-permute-start.4 = (bf16[2,256,1088]{1,2,0:T(8,128)(2,1)}, bf16[2,256,1088]{1,2,0:T(8,128)(2,1)}, u32[]{:S(2)}, u32[]{:S(2)}) collective-permute-start(bf16[2,256,1088]{1,2,0:T(8,128)(2,1)} %pad_maximum_fusion.5), channel_id=1, source_target_pairs={{0,1},{1,0},{2,3},{3,2},{4,5},{5,4},{6,7},{7,6},{8,9},{9,8},{10,11... | collective-permute-start | bytes 3342344 | tf_op jit(solution)/shard_map/ppermute | solution.py:46
  34.5 6.8 %copy-start.6 = (s32[4]{0:T(128)S(1)}, s32[4]{0:T(128)}, u32[]{:S(2)}) copy-start(s32[4]{0:T(128)} %constant.120.clone) | copy-start | bytes 52
  71.6 10.3 %copy-start.2 = (bf16[960,1024]{1,0:T(8,128)(2,1)}, bf16[960,1024]{1,0:T(8,128)(2,1)S(1)}, u32[]{:S(2)}) copy-start(bf16[960,1024]{1,0:T(8,128)(2,1)S(1)} %add_convert_fusion.1.q_ref.k_ref.v_ref) | copy-start | bytes 5898244
  71.6 10.3 %copy-start.36 = (bf16[272,1088]{1,0:T(8,128)(2,1)S(1)}, bf16[272,1088]{1,0:T(8,128)(2,1)}, u32[]{:S(2)}) copy-start(bf16[272,1088]{1,0:T(8,128)(2,1)} %param.22) | copy-start | bytes 1775620
  83.5 15.5 %collective-permute-start.7 = (bf16[2,256,1088]{1,2,0:T(8,128)(2,1)S(1)}, bf16[2,256,1088]{1,2,0:T(8,128)(2,1)S(1)}, u32[]{:S(2)}, u32[]{:S(2)}) collective-permute-start(bf16[2,256,1088]{1,2,0:T(8,128)(2,1)S(1)} %bitcast.186), channel_id=1, source_target_pairs={{0,1},{1,0},{2,3},{3,2},{4,5},{5,4},{6,7},{7,6},{8,9},{9,8},{10,11... | collective-permute-start | bytes 3342344 | tf_op jit(solution)/shard_map/ppermute | solution.py:46
  91.2 63.1 %collective-permute-start.11 = (bf16[1,272,1088]{2,1,0:T(8,128)(2,1)}, bf16[1,272,1088]{2,1,0:T(8,128)(2,1)}, u32[]{:S(2)}, u32[]{:S(2)}) collective-permute-start(bf16[1,272,1088]{2,1,0:T(8,128)(2,1)} %bitcast.161), channel_id=1, source_target_pairs={{0,1},{1,0},{2,3},{3,2},{4,5},{5,4},{6,7},{7,6},{8,9},{9,8},{10,11... | collective-permute-start | bytes 1775624 | tf_op jit(solution)/shard_map/ppermute | solution.py:46
  93.5 77.0 %collective-permute-start.12 = (bf16[1,272,1088]{2,1,0:T(8,128)(2,1)}, bf16[1,272,1088]{2,1,0:T(8,128)(2,1)}, u32[]{:S(2)}, u32[]{:S(2)}) collective-permute-start(bf16[1,272,1088]{2,1,0:T(8,128)(2,1)} %bitcast.160), channel_id=1, source_target_pairs={{0,2},{1,3},{2,0},{3,1},{4,6},{5,7},{6,4},{7,5},{8,10},{9,11},{10,... | collective-permute-start | bytes 1775624 | tf_op jit(solution)/shard_map/ppermute | solution.py:46
  94.7 78.8 %collective-permute-start.13 = (bf16[1,272,1088]{2,1,0:T(8,128)(2,1)}, bf16[1,272,1088]{2,1,0:T(8,128)(2,1)}, u32[]{:S(2)}, u32[]{:S(2)}) collective-permute-start(bf16[1,272,1088]{2,1,0:T(8,128)(2,1)} %bitcast.159), channel_id=1, source_target_pairs={{0,3},{1,2},{2,1},{3,0},{4,7},{5,6},{6,5},{7,4},{8,11},{9,10},{10,... | collective-permute-start | bytes 1775624 | tf_op jit(solution)/shard_map/ppermute | solution.py:46
  96.6 39.5 %collective-permute-start.16 = (bf16[1,256,1088]{1,2,0:T(8,128)(2,1)}, bf16[1,256,1088]{1,2,0:T(8,128)(2,1)}, u32[]{:S(2)}, u32[]{:S(2)}) collective-permute-start(bf16[1,256,1088]{1,2,0:T(8,128)(2,1)} %convert_element_type.265), channel_id=1, source_target_pairs={{0,2},{1,3},{2,0},{3,1},{4,6},{5,7},{6,4},{7,5},{8,10},{9,11},{10,... | collective-permute-start | bytes 1671176 | tf_op jit(solution)/shard_map/ppermute | solution.py:46
  100.2 46.9 %collective-permute-start.8 = (bf16[1,256,1088]{1,2,0:T(8,128)(2,1)}, bf16[1,256,1088]{1,2,0:T(8,128)(2,1)}, u32[]{:S(2)}, u32[]{:S(2)}) collective-permute-start(bf16[1,256,1088]{1,2,0:T(8,128)(2,1)} %slice.326), channel_id=1, source_target_pairs={{0,2},{1,3},{2,0},{3,1},{4,6},{5,7},{6,4},{7,5},{8,10},{9,11},{10,... | collective-permute-start | bytes 1671176 | tf_op jit(solution)/shard_map/ppermute | solution.py:46
  102.0 45.2 %copy-start.9 = (bf16[1,256,1088]{1,2,0:T(8,128)(2,1)S(1)}, bf16[1,256,1088]{1,2,0:T(8,128)(2,1)}, u32[]{:S(2)}) copy-start(bf16[1,256,1088]{1,2,0:T(8,128)(2,1)} %param.16) | copy-start | bytes 1671172
  138.4 11.7 %copy-start.15 = (f32[2,256,1088]{1,2,0:T(8,128)S(1)}, f32[2,256,1088]{1,2,0:T(8,128)}, u32[]{:S(2)}) copy-start(f32[2,256,1088]{1,2,0:T(8,128)} %copy-done.14) | copy-start | bytes 6684676
  138.4 37.1 %collective-permute-start.17 = (bf16[2,256,1088]{1,2,0:T(8,128)(2,1)}, bf16[2,256,1088]{1,2,0:T(8,128)(2,1)}, u32[]{:S(2)}, u32[]{:S(2)}) collective-permute-start(bf16[2,256,1088]{1,2,0:T(8,128)(2,1)} %pad_maximum_fusion.7), channel_id=1, source_target_pairs={{0,1},{1,0},{2,3},{3,2},{4,5},{5,4},{6,7},{7,6},{8,9},{9,8},{10,11... | collective-permute-start | bytes 3342344 | tf_op jit(solution)/shard_map/ppermute | solution.py:46
  152.9 14.0 %collective-permute-start.9 = (bf16[1,256,1088]{1,2,0:T(8,128)(2,1)}, bf16[1,256,1088]{1,2,0:T(8,128)(2,1)}, u32[]{:S(2)}, u32[]{:S(2)}) collective-permute-start(bf16[1,256,1088]{1,2,0:T(8,128)(2,1)} %get-tuple-element.55), channel_id=1, source_target_pairs={{0,2},{1,3},{2,0},{3,1},{4,6},{5,7},{6,4},{7,5},{8,10},{9,11},{10,... | collective-permute-start | bytes 1671176 | tf_op jit(solution)/shard_map/ppermute | solution.py:46
  154.3 132.4 %collective-permute-start.20 = (bf16[48,1088]{1,0:T(8,128)(2,1)S(1)}, bf16[48,1088]{1,0:T(8,128)(2,1)}, u32[]{:S(2)}, u32[]{:S(2)}) collective-permute-start(bf16[48,1088]{1,0:T(8,128)(2,1)S(1)} %get-tuple-element.92), channel_id=1, source_target_pairs={{0,1},{1,2},{2,3},{4,5},{5,6},{6,7},{8,9},{9,10},{10,11},{12,13},{... | collective-permute-start | bytes 313352 | tf_op jit(solution)/shard_map/ppermute | solution.py:353
  166.9 119.9 %collective-permute-start.21 = (bf16[48,1088]{1,0:T(8,128)(2,1)S(1)}, bf16[48,1088]{1,0:T(8,128)(2,1)}, u32[]{:S(2)}, u32[]{:S(2)}) collective-permute-start(bf16[48,1088]{1,0:T(8,128)(2,1)S(1)} %get-tuple-element.91), channel_id=1, source_target_pairs={{1,0},{2,1},{3,2},{5,4},{6,5},{7,6},{9,8},{10,9},{11,10},{13,12},{... | collective-permute-start | bytes 313352 | tf_op jit(solution)/shard_map/ppermute | solution.py:355
  170.5 22.3 %collective-permute-start.10 = (bf16[2,256,1088]{1,2,0:T(8,128)(2,1)}, bf16[2,256,1088]{1,2,0:T(8,128)(2,1)}, u32[]{:S(2)}, u32[]{:S(2)}) collective-permute-start(bf16[2,256,1088]{1,2,0:T(8,128)(2,1)} %pad_maximum_fusion.6), channel_id=1, source_target_pairs={{0,1},{1,0},{2,3},{3,2},{4,5},{5,4},{6,7},{7,6},{8,9},{9,8},{10,11... | collective-permute-start | bytes 3342344 | tf_op jit(solution)/shard_map/ppermute | solution.py:46
  200.1 6.4 %copy-start.30 = (bf16[4,256,1088]{2,1,0:T(8,128)(2,1)S(1)}, bf16[4,256,1088]{2,1,0:T(8,128)(2,1)}, u32[]{:S(2)}) copy-start(bf16[4,256,1088]{2,1,0:T(8,128)(2,1)} %copy.77) | copy-start | bytes 6684676
  206.5 5.0 copy-start.28
  214.7 6.6 %copy-start.21 = (f32[1024,1088]{0,1:T(8,128)}, f32[1024,1088]{0,1:T(8,128)S(1)}, u32[]{:S(2)}) copy-start(f32[1024,1088]{0,1:T(8,128)S(1)} %fusion.80) | copy-start | bytes 13369348
  214.9 6.4 %collective-permute-start.18 = (bf16[2,256,1088]{1,2,0:T(8,128)(2,1)S(1)}, bf16[2,256,1088]{1,2,0:T(8,128)(2,1)S(1)}, u32[]{:S(2)}, u32[]{:S(2)}) collective-permute-start(bf16[2,256,1088]{1,2,0:T(8,128)(2,1)S(1)} %bitcast.188), channel_id=1, source_target_pairs={{0,1},{1,0},{2,3},{3,2},{4,5},{5,4},{6,7},{7,6},{8,9},{9,8},{10,11... | collective-permute-start | bytes 3342344 | tf_op jit(solution)/shard_map/ppermute | solution.py:46
  218.5 7.1 %collective-permute-start.14 = (bf16[2,256,1088]{1,2,0:T(8,128)(2,1)S(1)}, bf16[2,256,1088]{1,2,0:T(8,128)(2,1)S(1)}, u32[]{:S(2)}, u32[]{:S(2)}) collective-permute-start(bf16[2,256,1088]{1,2,0:T(8,128)(2,1)S(1)} %bitcast.187), channel_id=1, source_target_pairs={{0,1},{1,0},{2,3},{3,2},{4,5},{5,4},{6,7},{7,6},{8,9},{9,8},{10,11... | collective-permute-start | bytes 3342344 | tf_op jit(solution)/shard_map/ppermute | solution.py:46
  223.3 15.7 %collective-permute-start.19 = (bf16[1,256,1088]{1,2,0:T(8,128)(2,1)S(1)}, bf16[1,256,1088]{1,2,0:T(8,128)(2,1)S(1)}, u32[]{:S(2)}, u32[]{:S(2)}) collective-permute-start(bf16[1,256,1088]{1,2,0:T(8,128)(2,1)S(1)} %slice.324), channel_id=1, source_target_pairs={{0,2},{1,3},{2,0},{3,1},{4,6},{5,7},{6,4},{7,5},{8,10},{9,11},{10,... | collective-permute-start | bytes 1671176 | tf_op jit(solution)/shard_map/ppermute | solution.py:46
  225.6 13.4 %copy-start.19 = (f32[256,1088]{0,1:T(8,128)S(1)}, f32[256,1088]{0,1:T(8,128)}, u32[]{:S(2)}) copy-start(f32[256,1088]{0,1:T(8,128)} %copy-done.18) | copy-start | bytes 3342340
  225.8 24.8 %copy-start.23 = (f32[1,256,1088]{1,2,0:T(8,128)S(1)}, f32[1,256,1088]{1,2,0:T(8,128)}, u32[]{:S(2)}) copy-start(f32[1,256,1088]{1,2,0:T(8,128)} %param.30) | copy-start | bytes 3342340
  225.9 24.8 %copy-start.25 = (f32[1,256,1088]{1,2,0:T(8,128)S(1)}, f32[1,256,1088]{1,2,0:T(8,128)}, u32[]{:S(2)}) copy-start(f32[1,256,1088]{1,2,0:T(8,128)} %get-tuple-element.56) | copy-start | bytes 3342340
  225.9 24.7 %collective-permute-start.15 = (bf16[1,256,1088]{1,2,0:T(8,128)(2,1)S(1)}, bf16[1,256,1088]{1,2,0:T(8,128)(2,1)S(1)}, u32[]{:S(2)}, u32[]{:S(2)}) collective-permute-start(bf16[1,256,1088]{1,2,0:T(8,128)(2,1)S(1)} %slice.325), channel_id=1, source_target_pairs={{0,2},{1,3},{2,0},{3,1},{4,6},{5,7},{6,4},{7,5},{8,10},{9,11},{10,... | collective-permute-start | bytes 1671176 | tf_op jit(solution)/shard_map/ppermute | solution.py:46
  252.6 15.5 %collective-permute-start.22 = (bf16[1,256,1088]{1,2,0:T(8,128)(2,1)S(1)}, bf16[1,256,1088]{1,2,0:T(8,128)(2,1)S(1)}, u32[]{:S(2)}, u32[]{:S(2)}) collective-permute-start(bf16[1,256,1088]{1,2,0:T(8,128)(2,1)S(1)} %get-tuple-element.53), channel_id=1, source_target_pairs={{0,2},{1,3},{2,0},{3,1},{4,6},{5,7},{6,4},{7,5},{8,10},{9,11},{10,... | collective-permute-start | bytes 1671176 | tf_op jit(solution)/shard_map/ppermute | solution.py:46
  259.3 13.3 %collective-permute-start.29 = (bf16[1,272,1088]{2,1,0:T(8,128)(2,1)S(1)}, bf16[1,272,1088]{2,1,0:T(8,128)(2,1)S(1)}, u32[]{:S(2)}, u32[]{:S(2)}) collective-permute-start(bf16[1,272,1088]{2,1,0:T(8,128)(2,1)S(1)} %get-tuple-element.64), channel_id=1, source_target_pairs={{0,1},{1,0},{2,3},{3,2},{4,5},{5,4},{6,7},{7,6},{8,9},{9,8},{10,11... | collective-permute-start | bytes 1775624 | tf_op jit(solution)/shard_map/ppermute | solution.py:46
  259.3 22.3 %collective-permute-start.30 = (bf16[1,272,1088]{2,1,0:T(8,128)(2,1)S(1)}, bf16[1,272,1088]{2,1,0:T(8,128)(2,1)S(1)}, u32[]{:S(2)}, u32[]{:S(2)}) collective-permute-start(bf16[1,272,1088]{2,1,0:T(8,128)(2,1)S(1)} %get-tuple-element.63), channel_id=1, source_target_pairs={{0,2},{1,3},{2,0},{3,1},{4,6},{5,7},{6,4},{7,5},{8,10},{9,11},{10,... | collective-permute-start | bytes 1775624 | tf_op jit(solution)/shard_map/ppermute | solution.py:46
  268.2 13.4 %collective-permute-start.23 = (bf16[2,256,1088]{1,2,0:T(8,128)(2,1)S(1)}, bf16[2,256,1088]{1,2,0:T(8,128)(2,1)S(1)}, u32[]{:S(2)}, u32[]{:S(2)}) collective-permute-start(bf16[2,256,1088]{1,2,0:T(8,128)(2,1)S(1)} %pad_maximum_fusion.8), channel_id=1, source_target_pairs={{0,1},{1,0},{2,3},{3,2},{4,5},{5,4},{6,7},{7,6},{8,9},{9,8},{10,11... | collective-permute-start | bytes 3342344 | tf_op jit(solution)/shard_map/ppermute | solution.py:46
  272.6 41.6 %collective-permute-start.31 = (bf16[1,272,1088]{2,1,0:T(8,128)(2,1)}, bf16[1,272,1088]{2,1,0:T(8,128)(2,1)}, u32[]{:S(2)}, u32[]{:S(2)}) collective-permute-start(bf16[1,272,1088]{2,1,0:T(8,128)(2,1)} %get-tuple-element.62), channel_id=1, source_target_pairs={{0,3},{1,2},{2,1},{3,0},{4,7},{5,6},{6,5},{7,4},{8,11},{9,10},{10,... | collective-permute-start | bytes 1775624 | tf_op jit(solution)/shard_map/ppermute | solution.py:46
  312.4 17.4 %collective-permute-start.26 = (bf16[1,272,816]{2,1,0:T(8,128)(2,1)}, bf16[1,272,816]{2,1,0:T(8,128)(2,1)}, u32[]{:S(2)}, u32[]{:S(2)}) collective-permute-start(bf16[1,272,816]{2,1,0:T(8,128)(2,1)} %get-tuple-element.76), channel_id=1, source_target_pairs={{0,1},{1,0},{2,3},{3,2},{4,5},{5,4},{6,7},{7,6},{8,9},{9,8},{10,11... | collective-permute-start | bytes 1331720 | tf_op jit(solution)/shard_map/ppermute | solution.py:46
  312.4 18.8 %collective-permute-start.27 = (bf16[1,272,816]{2,1,0:T(8,128)(2,1)}, bf16[1,272,816]{2,1,0:T(8,128)(2,1)}, u32[]{:S(2)}, u32[]{:S(2)}) collective-permute-start(bf16[1,272,816]{2,1,0:T(8,128)(2,1)} %get-tuple-element.75), channel_id=1, source_target_pairs={{0,2},{1,3},{2,0},{3,1},{4,6},{5,7},{6,4},{7,5},{8,10},{9,11},{10,... | collective-permute-start | bytes 1331720 | tf_op jit(solution)/shard_map/ppermute | solution.py:46
  323.3 13.5 %collective-permute-start.28 = (bf16[1,272,816]{2,1,0:T(8,128)(2,1)}, bf16[1,272,816]{2,1,0:T(8,128)(2,1)}, u32[]{:S(2)}, u32[]{:S(2)}) collective-permute-start(bf16[1,272,816]{2,1,0:T(8,128)(2,1)} %get-tuple-element.74), channel_id=1, source_target_pairs={{0,3},{1,2},{2,1},{3,0},{4,7},{5,6},{6,5},{7,4},{8,11},{9,10},{10,... | collective-permute-start | bytes 1331720 | tf_op jit(solution)/shard_map/ppermute | solution.py:46
  355.0 2.8 collective-permute-start.24
  357.8 44.5 %copy-start.10 = (bf16[1,256,1088]{1,2,0:T(8,128)(2,1)S(1)}, bf16[1,256,1088]{1,2,0:T(8,128)(2,1)}, u32[]{:S(2)}) copy-start(bf16[1,256,1088]{1,2,0:T(8,128)(2,1)} %param.16) | copy-start | bytes 1671172
  359.4 44.9 %copy-start.24 = (f32[1,256,1088]{1,2,0:T(8,128)S(1)}, f32[1,256,1088]{1,2,0:T(8,128)}, u32[]{:S(2)}) copy-start(f32[1,256,1088]{1,2,0:T(8,128)} %get-tuple-element.54) | copy-start | bytes 3342340
  359.5 42.8 %collective-permute-start.25 = (bf16[1,256,1088]{1,2,0:T(8,128)(2,1)S(1)}, bf16[1,256,1088]{1,2,0:T(8,128)(2,1)S(1)}, u32[]{:S(2)}, u32[]{:S(2)}) collective-permute-start(bf16[1,256,1088]{1,2,0:T(8,128)(2,1)S(1)} %slice.323), channel_id=1, source_target_pairs={{0,2},{1,3},{2,0},{3,1},{4,6},{5,7},{6,4},{7,5},{8,10},{9,11},{10,... | collective-permute-start | bytes 1671176 | tf_op jit(solution)/shard_map/ppermute | solution.py:46
  (29 other events, 79.3 us)
Sparse Core Ops, SparseCore 0:
  350.7 245.8 all-reduce.2

commit v2 on v1

--- a/solution.py
+++ b/solution.py
@@ -63,10 +63,9 @@
 
 
 def gather_relative(block):
-    stack = block[None]
     for bit in bits_far_first():
-        stack = jnp.concatenate([stack, swap(stack, bit)], axis=0)
-    return stack
+        block = jnp.concatenate([block, swap(block, bit)], axis=0)
+    return block
 
 
 def gather_absolute(block):
@@ -87,7 +86,41 @@
         half = parts.shape[0] // 2
         other = swap(parts[half:].astype(low), bit)
         parts = parts[:half] + other.astype(f32)
-    return parts[0]
+    return parts
+
+
+def swap_rep(values, bit):
+    size = lax.axis_size("rep")
+    return lax.ppermute(values, "rep", [(i, i ^ bit) for i in range(size)])
+
+
+def rep_bits(turned):
+    bits, bit = [], 1
+    while bit < lax.axis_size("rep"):
+        bits.append(bit)
+        bit *= 2
+    return bits[1:] + bits[:1] if turned else bits
+
+
+def rep_sum(values, turned=False, halvings=None):
+    bits = rep_bits(turned)
+    halvings = len(bits) if halvings is None else halvings
+    rows, cols = values.shape
+    index = lax.axis_index("rep")
+    total = values.reshape((2,) * halvings + (rows >> halvings, cols))
+    for bit in bits[:halvings]:
+        mine = (index // bit) % 2
+        send = lax.dynamic_index_in_dim(total, 1 - mine, 0, keepdims=False)
+        keep = lax.dynamic_index_in_dim(total, mine, 0, keepdims=False)
+        total = (keep.astype(f32) + swap_rep(send, bit).astype(f32)).astype(low)
+    for bit in bits[halvings:]:
+        total = (total.astype(f32) + swap_rep(total, bit).astype(f32)).astype(low)
+    total = lax.optimization_barrier(total)
+    for bit in reversed(bits[:halvings]):
+        upper = (index // bit) % 2 != 0
+        other = swap_rep(total, bit)
+        total = jnp.stack([jnp.where(upper, other, total), jnp.where(upper, total, other)])
+    return total.reshape(rows, cols)
 
 
 def exchange(blocks):
@@ -343,7 +376,7 @@
         )
     ).reshape(width, 3 * window)
     weight_up = exchange(
-        up_weight.reshape(own, shards, hidden).transpose(1, 0, 2)
+        jnp.stack([up_weight[:, s * hidden : (s + 1) * hidden] for s in range(shards)])
     ).reshape(width, hidden)
     to_right = [(i, i + 1) for i in range(shards - 1)]
     to_left = [(i + 1, i) for i in range(shards - 1)]
@@ -360,14 +393,14 @@
         window,
         0,
     )
-    branch_all = gather_relative(cotangent.reshape(seqs * span, width).astype(low))
+    branch = gather_relative(cotangent.reshape(seqs * span, width).astype(low))
     grad_out = cotangent.reshape(seqs * span, width)
 
     def own_rows(values):
         return lax.dynamic_slice_in_dim(values, skew, own, 0)
 
     rows = shards * seqs * span
-    normed_all, _ = normalize(inputs_all.reshape(rows, width).astype(f32))
+    normed_all, _ = normalize(inputs_all.astype(f32))
     hidden_one = (normed_all * gain_one + shift_one).astype(low)
     bias_window = jnp.concatenate(
         [
@@ -394,38 +427,35 @@
     forward_parts = [attend_forward(place, p, heads, span) for p in projected_parts]
     attended = own_rows(join_sequences([p[1] for p in forward_parts]))
     mixed_sum = scatter_relative(
-        contract(attended, attention_output_weight, 0, 0).reshape(shards, seqs * span, width)
+        contract(attended, attention_output_weight, 0, 0)
     )
     layer_input = own_input.astype(f32)
     middle = layer_input + mixed_sum + bias_out
 
     normed_two, inverse_two = normalize(middle)
-    hidden_two = gather_relative((normed_two * gain_two + shift_two).astype(low)).reshape(
-        rows, width
-    )
-    branch = branch_all.reshape(rows, width)
+    hidden_two = gather_relative((normed_two * gain_two + shift_two).astype(low))
     before = contract(hidden_two, weight_up, 1, 0) + up_bias
     activated, slope = gelu_parts(before)
     activated = activated.astype(low)
     grad_before = (contract(branch, down_weight, 1, 1) * slope).astype(low)
     grad_hidden_two = scatter_relative(
-        contract(grad_before, weight_up, 1, 1).reshape(shards, seqs * span, width)
-    )
-    down_weight_grad = lax.psum(contract(activated, branch, 0, 0).astype(low), "rep")
+        contract(grad_before, weight_up, 1, 1)
+    )
+    down_weight_grad = rep_sum(contract(activated, branch, 0, 0).astype(low))
     up_weight_grad = exchange(
         contract(hidden_two, grad_before, 0, 0).astype(low).reshape(shards, own, hidden)
     )
-    up_weight_grad = lax.psum(up_weight_grad, "rep")
+    up_weight_grad = rep_sum(up_weight_grad.reshape(width, hidden), turned=True)
     block_output = (
         middle
         + scatter_relative(
-            contract(activated, down_weight, 1, 0).reshape(shards, seqs * span, width)
+            contract(activated, down_weight, 1, 0)
         )
         + bias_down
     )
     grad_middle = grad_out + norm_back(grad_hidden_two, normed_two, inverse_two, gain_two)
 
-    grad_mixed = gather_relative(grad_middle.astype(low)).reshape(rows, width)
+    grad_mixed = gather_relative(grad_middle.astype(low))
     grad_attended = contract(weight_out_window, grad_mixed, 1, 1).astype(low)
     grad_parts = per_sequence(grad_attended) if seqs > 1 else [grad_attended]
     backward_parts = [
@@ -445,10 +475,20 @@
     input_weight_grad = exchange(
         contract(hidden_one, own_projected, 0, 1).astype(low).reshape(shards, own, 3 * own)
     )
-    input_weight_grad = lax.psum(input_weight_grad, "rep")
-    output_weight_grad = lax.psum(contract(attended, grad_mixed, 1, 0).astype(low), "rep")
+    input_weight_grad = input_weight_grad.reshape(width, 3 * own)
+    cut = (3 * own // 2) // 128 * 128
+    input_weight_grad = jnp.concatenate(
+        [
+            rep_sum(input_weight_grad[:, :cut]),
+            rep_sum(input_weight_grad[:, cut:], turned=True),
+        ],
+        axis=1,
+    )
+    output_weight_grad = rep_sum(
+        contract(attended, grad_mixed, 1, 0).astype(low), halvings=1
+    )
     grad_hidden_one = scatter_relative(
-        contract(grad_projected, weight_in, 0, 1).reshape(shards, seqs * span, width)
+        contract(grad_projected, weight_in, 0, 1)
     )
     normed_one, inverse_one = normalize(layer_input)
     input_grad = grad_middle + norm_back(grad_hidden_one, normed_one, inverse_one, gain_one)
@@ -456,52 +496,61 @@
     def own_part(values):
         return lax.dynamic_slice_in_dim(values, index * own, own, 0)
 
-    partial = lax.psum(
-        jnp.stack(
-            [
-                jnp.sum(grad_hidden_one * normed_one, axis=0),
-                jnp.sum(grad_hidden_one, axis=0),
-                jnp.sum(grad_hidden_two * normed_two, axis=0),
-                jnp.sum(grad_hidden_two, axis=0),
-            ]
-        ),
-        ("rep", "shard"),
-    )
-    first_gain_grad, first_shift_grad, second_gain_grad, second_shift_grad = (
-        own_part(partial[i]) for i in range(4)
-    )
-    complete = lax.psum(
-        jnp.concatenate(
-            [
-                jnp.sum(own_query.astype(f32), axis=1),
-                jnp.sum(own_value.astype(f32), axis=1),
-                own_part(jnp.sum(grad_mixed.astype(f32), axis=0)),
-                own_part(jnp.sum(branch.astype(f32), axis=0)),
-                jnp.sum(grad_before.astype(f32), axis=0),
-            ]
-        ),
-        "rep",
-    )
-    query_bias_grad, value_bias_grad, output_bias_grad, down_bias_grad = (
-        complete[i * own : (i + 1) * own] for i in range(4)
-    )
-    up_bias_grad = complete[4 * own :]
+    partial = jnp.stack(
+        [
+            jnp.sum(grad_hidden_one * normed_one, axis=0),
+            jnp.sum(grad_hidden_one, axis=0),
+            jnp.sum(grad_hidden_two * normed_two, axis=0),
+            jnp.sum(grad_hidden_two, axis=0),
+        ]
+    )
+    for bit in bits_far_first():
+        partial = partial + swap(partial, bit)
+    complete = jnp.concatenate(
+        [own_part(partial[i]) for i in range(4)]
+        + [
+            jnp.sum(own_query.astype(f32), axis=1),
+            jnp.sum(own_value.astype(f32), axis=1),
+            own_part(jnp.sum(grad_mixed.astype(f32), axis=0)),
+            own_part(jnp.sum(branch.astype(f32), axis=0)),
+            jnp.sum(grad_before.astype(f32), axis=0),
+        ]
+    )
+    for bit in rep_bits(False):
+        complete = complete + swap_rep(complete, bit)
+    (
+        first_gain_grad,
+        first_shift_grad,
+        second_gain_grad,
+        second_shift_grad,
+        query_bias_grad,
+        value_bias_grad,
+        output_bias_grad,
+        down_bias_grad,
+    ) = (complete[i * own : (i + 1) * own] for i in range(8))
+    up_bias_grad = complete[8 * own :]
     return (
         block_output.reshape(seqs, span, width),
         input_grad.reshape(seqs, span, width),
         first_gain_grad,
         first_shift_grad,
-        input_weight_grad.reshape(shards, own, 3, own)
-        .transpose(1, 2, 0, 3)
-        .reshape(own, 3 * width)
-        .astype(f32),
+        jnp.concatenate(
+            [
+                input_weight_grad[s * own : (s + 1) * own, part * own : (part + 1) * own]
+                for part in range(3)
+                for s in range(shards)
+            ],
+            axis=1,
+        ).astype(f32),
         query_bias_grad,
         value_bias_grad,
         output_weight_grad.astype(f32),
         output_bias_grad,
         second_gain_grad,
         second_shift_grad,
-        up_weight_grad.transpose(1, 0, 2).reshape(own, shards * hidden).astype(f32),
+        jnp.concatenate(
+            [up_weight_grad[s * own : (s + 1) * own] for s in range(shards)], axis=1
+        ).astype(f32),
         up_bias_grad,
         down_weight_grad.astype(f32),
         down_bias_grad,

time: 619 us -> 520 us (0.84)
  blocking collectives: 80.5 us -> 0 us
  local copies, waits for them, and re-layouts: 119 us -> 53.7 us
  starting transfers between devices: 27.9 us -> 66.8 us
  waiting for transfers between devices: 251 us -> 264 us
  between operations: 15.2 us -> 2.31 us
    ppermute x0 -> x31, waiting for transfers between devices: none -> 164 us  [swap_rep(): return lax.ppermute(values, 'rep', [(i, i ^ bit) for i in range(size)])]
    psum x1 -> x0, waiting for transfers between devices: 148 us -> none  [local(): input_weight_grad = lax.psum(input_weight_grad, 'rep')]
    psum x2 -> x0, blocking collectives: 80.5 us -> none  [the longest x1 40.6 us: local(): lax.psum(jnp.stack([jnp.sum(grad_hidden_one * normed_one, axis=0), jnp.su...]
    ppermute x0 -> x31, starting transfers between devices: none -> 43.2 us  [swap_rep(): return lax.ppermute(values, 'rep', [(i, i ^ bit) for i in range(size)])]
    convert_element_type x10 -> x1, local copies, waits for them, and re-layouts: 25.6 us -> 0.08 us  [local(): middle + scatter_relative(contract(activated, down_weight, 1, 0))]
    another operation x0 -> x27, other arithmetic: none -> 13.6 us  [the longest x26 13.2 us: rep_sum(): jnp.stack([jnp.where(upper, other, total), jnp.where(upper, total, other)])]
    convert_element_type x7 -> x18, other arithmetic: 14.8 us -> 4.83 us  [the longest x1 1.94 us: local(): grad_mixed = gather_relative(grad_middle.astype(low))]
    reshape x1 -> x0, local copies, waits for them, and re-layouts: 6.8 us -> none  [local(): up_weight.reshape(own, shards, hidden).transpose(1, 0, 2)]
  transfers between devices with their start and end apart: 33 -> 65, of which waited for: 12 -> 27; matrix products, arithmetic and copies ran while one was open for 26% -> 25% of each run, Pallas kernels for 2% -> 2%
where the time goes in v2:
time: 520 us; the launch traced here: 513 us
  waiting for transfers between devices  264 us (51%)
  starting transfers between devices  66.8 us (13%)
  other arithmetic  60.7 us (12%)
  local copies, waits for them, and re-layouts  53.7 us (10%)
  matrix products  44.3 us (9%)
  Pallas kernels  21 us (4%)
    ppermute x31, waiting for transfers between devices, swap_rep(): return lax.ppermute(values, 'rep', [(i, i ^ bit) for i in range(size)])  164 us
    ppermute x32, waiting for transfers between devices, swap(): return lax.ppermute(values, 'shard', [(i, i ^ bit) for i in range(size)])  99.8 us
    dot_general x12, matrix products, contract(): lax.dot_general(left, right, (((left_dim,), (right_dim,)), ((), ())), pre...  44.3 us
    ppermute x31, starting transfers between devices, swap_rep(): return lax.ppermute(values, 'rep', [(i, i ^ bit) for i in range(size)])  43.2 us
    ppermute x32, starting transfers between devices, swap(): return lax.ppermute(values, 'shard', [(i, i ^ bit) for i in range(size)])  20.9 us
    another operation x26, other arithmetic, rep_sum(): jnp.stack([jnp.where(upper, other, total), jnp.where(upper, total, other)])  13.2 us
    dynamic_update_slice x12, local copies, waits for them, and re-layouts, exchange(): result = lax.dynamic_update_slice_in_dim(result, piece, peer, 0)  11.9 us
    pallas_call x1, Pallas kernels, attend_backward(): pl.pallas_call(functools.partial(backward_kernel, blocks, block), grid_sp...  10.6 us
  transfers between devices with their start and end apart: 65, of which 27 were waited for; matrix products, arithmetic and copies ran while one was open for 25% of the time, Pallas kernels for 2%

profile of v2, /device:TPU:0, one launch (start us, length us, event | category | flops | bytes accessed | tf_op | source)
XLA Modules:
  0.0 512.6 jit_solution(8682660247384320630)
XLA Ops:
  6.9 2.9 collective-permute-start.5
  9.9 3.2 fusion.86
  21.4 4.3 collective-permute-done.3
  31.2 6.4 %collective-permute-done.1 = bf16[1,272,960]{2,1,0:T(8,128)(2,1)} collective-permute-done((bf16[1,272,960]{2,1,0:T(8,128)(2,1)}, bf16[1,272,960]{2,1,0:T(8,128)(2,1)}, u32[]{:S(2)}, u32[]{:S(2)}) %collective-permute-start.1) | collective-permute-done | bytes 522272 | tf_op jit(solution)/shard_map/ppermute | solution.py:46
  39.5 7.1 %collective-permute-done.2 = bf16[1,272,960]{2,1,0:T(8,128)(2,1)} collective-permute-done((bf16[1,272,960]{2,1,0:T(8,128)(2,1)}, bf16[1,272,960]{2,1,0:T(8,128)(2,1)}, u32[]{:S(2)}, u32[]{:S(2)}) %collective-permute-start.2) | collective-permute-done | bytes 522272 | tf_op jit(solution)/shard_map/ppermute | solution.py:46
  52.5 4.5 add_convert_fusion.q_ref.k_ref.v_ref
  57.1 10.4 %attend_forward.1 = (f32[320,1024]{1,0:T(8,128)S(1)}, bf16[320,1024]{1,0:T(8,128)(2,1)S(1)}, f32[5,1,1024]{2,1,0:T(1,128)S(1)}) custom-call(s32[4]{0:T(128)S(1)} %gather_fusion, bf16[960,1024]{1,0:T(8,128)(2,1)S(1)} %add_convert_fusion.q_ref.k_ref.v_ref, bf16[960,1024]{1,0:T(8,128)(2,1)S(1)} %add_convert_fusion.q_ref.k_ref.v_ref, ...), custom_call_target="tpu_custom_call" | custom-call | flops 1342177280 | bytes 3932160 | tf_op jit(solution)/shard_map/attend_forward/pallas_call | solution.py:239
  79.7 36.6 %collective-permute-done.8 = bf16[256,1088]{0,1:T(8,128)(2,1)} collective-permute-done((bf16[256,1088]{0,1:T(8,128)(2,1)}, bf16[256,1088]{0,1:T(8,128)(2,1)}, u32[]{:S(2)}, u32[]{:S(2)}) %collective-permute-start.8) | collective-permute-done | bytes 557088 | tf_op jit(solution)/shard_map/ppermute | solution.py:46
  122.4 5.8 %collective-permute-done.16 = bf16[256,1088]{0,1:T(8,128)(2,1)} collective-permute-done((bf16[256,1088]{0,1:T(8,128)(2,1)}, bf16[256,1088]{0,1:T(8,128)(2,1)}, u32[]{:S(2)}, u32[]{:S(2)}) %collective-permute-start.16) | collective-permute-done | bytes 557088 | tf_op jit(solution)/shard_map/ppermute | solution.py:46
  128.3 2.3 pad_maximum_fusion.12
  131.1 8.1 %collective-permute-done.9 = bf16[256,1088]{0,1:T(8,128)(2,1)} collective-permute-done((bf16[256,1088]{0,1:T(8,128)(2,1)}, bf16[256,1088]{0,1:T(8,128)(2,1)}, u32[]{:S(2)}, u32[]{:S(2)}) %collective-permute-start.9) | collective-permute-done | bytes 557088 | tf_op jit(solution)/shard_map/ppermute | solution.py:46
  151.5 5.9 %multiply_convert_fusion = (bf16[1024,1088]{0,1:T(8,128)(2,1)S(1)}, f32[1024,1088]{0,1:T(8,128)S(1)}) fusion(f32[1088]{0:T(1024)S(1)} %convert_element_type.371, bf16[1088,1088]{1,0:T(8,128)(2,1)} %bitcast.224, bf16[512,1088]{0,1:T(8,128)(2,1)S(1)} %collective-permute-done.10, bf16[256,1088]{0,1:T(8,128)(2,1)} %collective-permute-done.9, ...), kind=kOutput, calls=%fused_computation.21 | convolution fusion | flops 2437677056 | bytes 11284736 | tf_op jit(solution)/shard_map/dot_general | solution.py:39
  157.4 7.4 %convert_reduce_fusion.1 = (f32[1088]{0:T(1024)}, bf16[1024,1088]{0,1:T(8,128)(2,1)S(1)}) fusion(f32[1024,1088]{0,1:T(8,128)S(1)} %get-tuple-element.153, bf16[1088,1088]{1,0:T(8,128)(2,1)S(1)} %copy-done, bf16[512,1088]{0,1:T(8,128)(2,1)} %collective-permute-done.17, bf16[256,1088]{0,1:T(8,128)(2,1)} %collective-permute-done.16, ...), kind=kOutput, calls=%fused_computation.18 | convolution fusion | flops 2444360704 | bytes 11284736 | tf_op jit(solution)/shard_map/dot_general | solution.py:39
  164.8 3.1 fusion.92
  168.2 3.1 fusion.91
  171.3 4.3 convolution_convert_fusion.1
  178.2 4.9 convolution_convert_fusion
  184.9 8.8 %collective-permute-done.51 = bf16[1,272,1088]{2,1,0:T(8,128)(2,1)S(1)} collective-permute-done((bf16[1,272,1088]{2,1,0:T(8,128)(2,1)S(1)}, bf16[1,272,1088]{2,1,0:T(8,128)(2,1)S(1)}, u32[]{:S(2)}, u32[]{:S(2)}) %collective-permute-start.51) | collective-permute-done | bytes 591904 | tf_op jit(solution)/shard_map/ppermute | solution.py:46
  193.8 11.6 %collective-permute-done.52 = bf16[1,272,1088]{2,1,0:T(8,128)(2,1)S(1)} collective-permute-done((bf16[1,272,1088]{2,1,0:T(8,128)(2,1)S(1)}, bf16[1,272,1088]{2,1,0:T(8,128)(2,1)S(1)}, u32[]{:S(2)}, u32[]{:S(2)}) %collective-permute-start.52) | collective-permute-done | bytes 591904 | tf_op jit(solution)/shard_map/ppermute | solution.py:46
  210.7 24.8 %collective-permute-done.59 = bf16[2,2,136,1088]{3,2,1,0:T(8,128)(2,1)S(1)} collective-permute-done((bf16[2,2,136,1088]{3,2,1,0:T(8,128)(2,1)S(1)}, bf16[2,2,136,1088]{3,2,1,0:T(8,128)(2,1)S(1)}, u32[]{:S(2)}, u32[]{:S(2)}) %collective-permute-start.59) | collective-permute-done | bytes 1183776 | tf_op jit(solution)/shard_map/ppermute | solution.py:94
  238.8 13.1 %collective-permute-done.60 = bf16[2,136,1088]{2,1,0:T(8,128)(2,1)S(1)} collective-permute-done((bf16[2,136,1088]{2,1,0:T(8,128)(2,1)S(1)}, bf16[2,136,1088]{2,1,0:T(8,128)(2,1)S(1)}, u32[]{:S(2)}, u32[]{:S(2)}) %collective-permute-start.60) | collective-permute-done | bytes 591904 | tf_op jit(solution)/shard_map/ppermute | solution.py:94
  252.1 2.8 collective-permute-start.61
  255.5 26.9 %collective-permute-done.61 = bf16[136,1088]{1,0:T(8,128)(2,1)S(1)} collective-permute-done((bf16[136,1088]{1,0:T(8,128)(2,1)S(1)}, bf16[136,1088]{1,0:T(8,128)(2,1)S(1)}, u32[]{:S(2)}, u32[]{:S(2)}) %collective-permute-start.61) | collective-permute-done | bytes 295968 | tf_op jit(solution)/shard_map/ppermute | solution.py:94
  286.4 21.7 %collective-permute-done.62 = bf16[136,1088]{1,0:T(8,128)(2,1)S(1)} collective-permute-done((bf16[136,1088]{1,0:T(8,128)(2,1)S(1)}, bf16[136,1088]{1,0:T(8,128)(2,1)S(1)}, u32[]{:S(2)}, u32[]{:S(2)}) %collective-permute-start.62) | collective-permute-done | bytes 295968 | tf_op jit(solution)/shard_map/ppermute | solution.py:94
  311.1 5.7 %collective-permute-done.55 = bf16[136,1088]{1,0:T(8,128)(2,1)S(1)} collective-permute-done((bf16[136,1088]{1,0:T(8,128)(2,1)S(1)}, bf16[136,1088]{1,0:T(8,128)(2,1)S(1)}, u32[]{:S(2)}, u32[]{:S(2)}) %collective-permute-start.55) | collective-permute-done | bytes 295968 | tf_op jit(solution)/shard_map/ppermute | solution.py:94
  318.5 6.4 %collective-permute-done.63 = bf16[2,136,1088]{2,1,0:T(8,128)(2,1)S(1)} collective-permute-done((bf16[2,136,1088]{2,1,0:T(8,128)(2,1)S(1)}, bf16[2,136,1088]{2,1,0:T(8,128)(2,1)S(1)}, u32[]{:S(2)}, u32[]{:S(2)}) %collective-permute-start.63) | collective-permute-done | bytes 591904 | tf_op jit(solution)/shard_map/ppermute | solution.py:94
  328.5 3.4 collective-permute-start.57
  333.1 10.6 %attend_backward.1 = (bf16[320,1024]{1,0:T(8,128)(2,1)S(1)}, bf16[320,1024]{1,0:T(8,128)(2,1)S(1)}, bf16[320,1024]{1,0:T(8,128)(2,1)S(1)}) custom-call(s32[4]{0:T(128)S(1)} %gather_fusion, bf16[960,1024]{1,0:T(8,128)(2,1)S(1)} %copy-done.3, bf16[960,1024]{1,0:T(8,128)(2,1)S(1)} %copy-done.3, bf16[960,1024]{1,0:T(8,128)(2,1)S(1)} %copy-done.3, ...), custom_call_target="tpu_custom_call" | custom-call | flops 3355443200 | bytes 6553600 | tf_op jit(solution)/shard_map/attend_backward/pallas_call | solution.py:276
  346.4 2.5 fusion.13
  352.0 5.1 %convolution_convert_fusion.2 = bf16[1088,816]{0,1:T(8,128)(2,1)} fusion(bf16[272,1024]{1,0:T(8,128)(2,1)S(1)} %get-tuple-element.44, bf16[272,1024]{1,0:T(8,128)(2,1)S(1)} %constant_dynamic-slice_fusion.6, bf16[272,1024]{1,0:T(8,128)(2,1)S(1)} %get-tuple-element.46, f32[1088]{0:T(1024)S(1)} %copy-done.45, f32[1088]{0:T(1024)S(1)} %reshape.293, ...), kind=kOutput, calls=%fused_computation.25 | convolution fusion | flops 1836387328 | bytes 5691904 | tf_op jit(solution)/shard_map/dot_general | solution.py:39
  357.1 3.4 copy.32
  366.8 6.6 %collective-permute-done.46 = bf16[136,1088]{1,0:T(8,128)(2,1)S(1)} collective-permute-done((bf16[136,1088]{1,0:T(8,128)(2,1)S(1)}, bf16[136,1088]{1,0:T(8,128)(2,1)S(1)}, u32[]{:S(2)}, u32[]{:S(2)}) %collective-permute-start.46) | collective-permute-done | bytes 295968 | tf_op jit(solution)/shard_map/ppermute | solution.py:94
  376.4 10.0 %collective-permute-done.33 = bf16[1,272,816]{2,1,0:T(8,128)(2,1)S(1)} collective-permute-done((bf16[1,272,816]{2,1,0:T(8,128)(2,1)S(1)}, bf16[1,272,816]{2,1,0:T(8,128)(2,1)S(1)}, u32[]{:S(2)}, u32[]{:S(2)}) %collective-permute-start.33) | collective-permute-done | bytes 443936 | tf_op jit(solution)/shard_map/ppermute | solution.py:46
  388.5 22.2 %collective-permute-done.47 = bf16[136,1088]{1,0:T(8,128)(2,1)S(1)} collective-permute-done((bf16[136,1088]{1,0:T(8,128)(2,1)S(1)}, bf16[136,1088]{1,0:T(8,128)(2,1)S(1)}, u32[]{:S(2)}, u32[]{:S(2)}) %collective-permute-start.47) | collective-permute-done | bytes 295968 | tf_op jit(solution)/shard_map/ppermute | solution.py:94
  415.4 2.8 bitcast_convert_fusion
  418.2 3.9 collective-permute-done.34
  423.9 4.6 collective-permute-done.48
  430.4 3.4 collective-permute-start.41
  434.0 2.9 collective-permute-start.36
  439.5 9.5 %collective-permute-done.41 = bf16[2,136,432]{2,1,0:T(8,128)(2,1)S(1)} collective-permute-done((bf16[2,136,432]{2,1,0:T(8,128)(2,1)S(1)}, bf16[2,136,432]{2,1,0:T(8,128)(2,1)S(1)}, u32[]{:S(2)}, u32[]{:S(2)}) %collective-permute-start.41) | collective-permute-done | bytes 235040 | tf_op jit(solution)/shard_map/ppermute | solution.py:94
  461.8 3.5 concatenate.87
  465.3 4.3 convert_element_type.442
  478.8 2.2 collective-permute-start.45
  482.2 3.2 collective-permute-done.28
  485.7 9.2 %collective-permute-done.29 = f32[3264]{0:T(1024)S(1)} collective-permute-done((f32[3264]{0:T(1024)S(1)}, f32[3264]{0:T(1024)S(1)}, u32[]{:S(2)}, u32[]{:S(2)}) %collective-permute-start.29) | collective-permute-done | bytes 13088 | tf_op jit(solution)/shard_map/ppermute | solution.py:94
  496.8 2.8 fusion.35
  504.2 4.6 concatenate.86
  508.8 3.5 convert_element_type.415
  (392 shorter events, 143.7 us)
Async XLA Ops:
  6.9 13.7 %collective-permute-start.5 = (bf16[1,8,272]{2,1,0:T(8,128)(2,1)}, bf16[1,8,272]{2,1,0:T(8,128)(2,1)}, u32[]{:S(2)}, u32[]{:S(2)}) collective-permute-start(bf16[1,8,272]{2,1,0:T(8,128)(2,1)} %bitcast.7), channel_id=1, source_target_pairs={{0,2},{1,3},{2,0},{3,1},{4,6},{5,7},{6,4},{7,5},{8,10},{9,11},{10,... | collective-permute-start | bytes 13064 | tf_op jit(solution)/shard_map/ppermute | solution.py:46
  9.8 15.9 %collective-permute-start.3 = (bf16[256,1088]{0,1:T(8,128)(2,1)}, bf16[256,1088]{0,1:T(8,128)(2,1)}, u32[]{:S(2)}, u32[]{:S(2)}) collective-permute-start(bf16[256,1088]{0,1:T(8,128)(2,1)} %bitcast.203), channel_id=1, source_target_pairs={{0,2},{1,3},{2,0},{3,1},{4,6},{5,7},{6,4},{7,5},{8,10},{9,11},{10,... | collective-permute-start | bytes 1671176 | tf_op jit(solution)/shard_map/ppermute | solution.py:46
  18.4 19.2 %collective-permute-start.1 = (bf16[1,272,960]{2,1,0:T(8,128)(2,1)}, bf16[1,272,960]{2,1,0:T(8,128)(2,1)}, u32[]{:S(2)}, u32[]{:S(2)}) collective-permute-start(bf16[1,272,960]{2,1,0:T(8,128)(2,1)} %get-tuple-element.72), channel_id=1, source_target_pairs={{0,2},{1,3},{2,0},{3,1},{4,6},{5,7},{6,4},{7,5},{8,10},{9,11},{10,... | collective-permute-start | bytes 1566728 | tf_op jit(solution)/shard_map/ppermute | solution.py:46
  20.4 26.2 %collective-permute-start.2 = (bf16[1,272,960]{2,1,0:T(8,128)(2,1)}, bf16[1,272,960]{2,1,0:T(8,128)(2,1)}, u32[]{:S(2)}, u32[]{:S(2)}) collective-permute-start(bf16[1,272,960]{2,1,0:T(8,128)(2,1)} %get-tuple-element.71), channel_id=1, source_target_pairs={{0,3},{1,2},{2,1},{3,0},{4,7},{5,6},{6,5},{7,4},{8,11},{9,10},{10,... | collective-permute-start | bytes 1566728 | tf_op jit(solution)/shard_map/ppermute | solution.py:46
  27.8 20.7 %collective-permute-start.4 = (bf16[512,1088]{0,1:T(8,128)(2,1)}, bf16[512,1088]{0,1:T(8,128)(2,1)}, u32[]{:S(2)}, u32[]{:S(2)}) collective-permute-start(bf16[512,1088]{0,1:T(8,128)(2,1)} %pad_maximum_fusion.10), channel_id=1, source_target_pairs={{0,1},{1,0},{2,3},{3,2},{4,5},{5,4},{6,7},{7,6},{8,9},{9,8},{10,11... | collective-permute-start | bytes 3342344 | tf_op jit(solution)/shard_map/ppermute | solution.py:46
  73.2 68.7 %collective-permute-start.11 = (bf16[1,272,1088]{2,1,0:T(8,128)(2,1)}, bf16[1,272,1088]{2,1,0:T(8,128)(2,1)}, u32[]{:S(2)}, u32[]{:S(2)}) collective-permute-start(bf16[1,272,1088]{2,1,0:T(8,128)(2,1)} %get-tuple-element.65), channel_id=1, source_target_pairs={{0,1},{1,0},{2,3},{3,2},{4,5},{5,4},{6,7},{7,6},{8,9},{9,8},{10,11... | collective-permute-start | bytes 1775624 | tf_op jit(solution)/shard_map/ppermute | solution.py:46
  73.7 71.4 %collective-permute-start.12 = (bf16[1,272,1088]{2,1,0:T(8,128)(2,1)}, bf16[1,272,1088]{2,1,0:T(8,128)(2,1)}, u32[]{:S(2)}, u32[]{:S(2)}) collective-permute-start(bf16[1,272,1088]{2,1,0:T(8,128)(2,1)} %get-tuple-element.64), channel_id=1, source_target_pairs={{0,2},{1,3},{2,0},{3,1},{4,6},{5,7},{6,4},{7,5},{8,10},{9,11},{10,... | collective-permute-start | bytes 1775624 | tf_op jit(solution)/shard_map/ppermute | solution.py:46
  74.1 72.9 %collective-permute-start.13 = (bf16[1,272,1088]{2,1,0:T(8,128)(2,1)}, bf16[1,272,1088]{2,1,0:T(8,128)(2,1)}, u32[]{:S(2)}, u32[]{:S(2)}) collective-permute-start(bf16[1,272,1088]{2,1,0:T(8,128)(2,1)} %get-tuple-element.63), channel_id=1, source_target_pairs={{0,3},{1,2},{2,1},{3,0},{4,7},{5,6},{6,5},{7,4},{8,11},{9,10},{10,... | collective-permute-start | bytes 1775624 | tf_op jit(solution)/shard_map/ppermute | solution.py:46
  76.3 40.0 %collective-permute-start.8 = (bf16[256,1088]{0,1:T(8,128)(2,1)}, bf16[256,1088]{0,1:T(8,128)(2,1)}, u32[]{:S(2)}, u32[]{:S(2)}) collective-permute-start(bf16[256,1088]{0,1:T(8,128)(2,1)} %slice.436), channel_id=1, source_target_pairs={{0,2},{1,3},{2,0},{3,1},{4,6},{5,7},{6,4},{7,5},{8,10},{9,11},{10,... | collective-permute-start | bytes 1671176 | tf_op jit(solution)/shard_map/ppermute | solution.py:46
  77.9 50.4 %collective-permute-start.16 = (bf16[256,1088]{0,1:T(8,128)(2,1)}, bf16[256,1088]{0,1:T(8,128)(2,1)}, u32[]{:S(2)}, u32[]{:S(2)}) collective-permute-start(bf16[256,1088]{0,1:T(8,128)(2,1)} %bitcast_convert_fusion.1), channel_id=1, source_target_pairs={{0,2},{1,3},{2,0},{3,1},{4,6},{5,7},{6,4},{7,5},{8,10},{9,11},{10,... | collective-permute-start | bytes 1671176 | tf_op jit(solution)/shard_map/ppermute | solution.py:46
  120.4 18.9 %collective-permute-start.9 = (bf16[256,1088]{0,1:T(8,128)(2,1)}, bf16[256,1088]{0,1:T(8,128)(2,1)}, u32[]{:S(2)}, u32[]{:S(2)}) collective-permute-start(bf16[256,1088]{0,1:T(8,128)(2,1)} %add_convert_fusion.1), channel_id=1, source_target_pairs={{0,2},{1,3},{2,0},{3,1},{4,6},{5,7},{6,4},{7,5},{8,10},{9,11},{10,... | collective-permute-start | bytes 1671176 | tf_op jit(solution)/shard_map/ppermute | solution.py:46
  130.5 18.4 %collective-permute-start.17 = (bf16[512,1088]{0,1:T(8,128)(2,1)}, bf16[512,1088]{0,1:T(8,128)(2,1)}, u32[]{:S(2)}, u32[]{:S(2)}) collective-permute-start(bf16[512,1088]{0,1:T(8,128)(2,1)} %pad_maximum_fusion.12), channel_id=1, source_target_pairs={{0,1},{1,0},{2,3},{3,2},{4,5},{5,4},{6,7},{7,6},{8,9},{9,8},{10,11... | collective-permute-start | bytes 3342344 | tf_op jit(solution)/shard_map/ppermute | solution.py:46
  139.3 192.6 %collective-permute-start.20 = (bf16[48,1088]{1,0:T(8,128)(2,1)}, bf16[48,1088]{1,0:T(8,128)(2,1)S(1)}, u32[]{:S(2)}, u32[]{:S(2)}) collective-permute-start(bf16[48,1088]{1,0:T(8,128)(2,1)} %get-tuple-element.123), channel_id=1, source_target_pairs={{0,1},{1,2},{2,3},{4,5},{5,6},{6,7},{8,9},{9,10},{10,11},{12,13},{... | collective-permute-start | bytes 313352 | tf_op jit(solution)/shard_map/ppermute | solution.py:386
  168.1 39.2 %collective-permute-start.18 = (bf16[512,1088]{0,1:T(8,128)(2,1)S(1)}, bf16[512,1088]{0,1:T(8,128)(2,1)S(1)}, u32[]{:S(2)}, u32[]{:S(2)}) collective-permute-start(bf16[512,1088]{0,1:T(8,128)(2,1)S(1)} %slice.430), channel_id=1, source_target_pairs={{0,1},{1,0},{2,3},{3,2},{4,5},{5,4},{6,7},{7,6},{8,9},{9,8},{10,11... | collective-permute-start | bytes 3342344 | tf_op jit(solution)/shard_map/ppermute | solution.py:46
  176.7 17.0 %collective-permute-start.51 = (bf16[1,272,1088]{2,1,0:T(8,128)(2,1)S(1)}, bf16[1,272,1088]{2,1,0:T(8,128)(2,1)S(1)}, u32[]{:S(2)}, u32[]{:S(2)}) collective-permute-start(bf16[1,272,1088]{2,1,0:T(8,128)(2,1)S(1)} %get-tuple-element.60), channel_id=1, source_target_pairs={{0,2},{1,3},{2,0},{3,1},{4,6},{5,7},{6,4},{7,5},{8,10},{9,11},{10,... | collective-permute-start | bytes 1775624 | tf_op jit(solution)/shard_map/ppermute | solution.py:46
  176.7 28.7 %collective-permute-start.52 = (bf16[1,272,1088]{2,1,0:T(8,128)(2,1)S(1)}, bf16[1,272,1088]{2,1,0:T(8,128)(2,1)S(1)}, u32[]{:S(2)}, u32[]{:S(2)}) collective-permute-start(bf16[1,272,1088]{2,1,0:T(8,128)(2,1)S(1)} %get-tuple-element.59), channel_id=1, source_target_pairs={{0,3},{1,2},{2,1},{3,0},{4,7},{5,6},{6,5},{7,4},{8,11},{9,10},{10,... | collective-permute-start | bytes 1775624 | tf_op jit(solution)/shard_map/ppermute | solution.py:46
  183.4 148.6 %collective-permute-start.21 = (bf16[48,1088]{1,0:T(8,128)(2,1)}, bf16[48,1088]{1,0:T(8,128)(2,1)S(1)}, u32[]{:S(2)}, u32[]{:S(2)}) collective-permute-start(bf16[48,1088]{1,0:T(8,128)(2,1)} %get-tuple-element.122), channel_id=1, source_target_pairs={{1,0},{2,1},{3,2},{5,4},{6,5},{7,6},{9,8},{10,9},{11,10},{13,12},{... | collective-permute-start | bytes 313352 | tf_op jit(solution)/shard_map/ppermute | solution.py:388
  193.7 15.8 %collective-permute-start.14 = (bf16[512,1088]{0,1:T(8,128)(2,1)S(1)}, bf16[512,1088]{0,1:T(8,128)(2,1)S(1)}, u32[]{:S(2)}, u32[]{:S(2)}) collective-permute-start(bf16[512,1088]{0,1:T(8,128)(2,1)S(1)} %slice.431), channel_id=1, source_target_pairs={{0,1},{1,0},{2,3},{3,2},{4,5},{5,4},{6,7},{7,6},{8,9},{9,8},{10,11... | collective-permute-start | bytes 3342344 | tf_op jit(solution)/shard_map/ppermute | solution.py:46
  205.4 30.2 %collective-permute-start.59 = (bf16[2,2,136,1088]{3,2,1,0:T(8,128)(2,1)S(1)}, bf16[2,2,136,1088]{3,2,1,0:T(8,128)(2,1)S(1)}, u32[]{:S(2)}, u32[]{:S(2)}) collective-permute-start(bf16[2,2,136,1088]{3,2,1,0:T(8,128)(2,1)S(1)} %dynamic-slice_bitcast_fusion), channel_id=1, source_target_pairs={{0,4},{4,0},{8,12},{12,8},{16,20},{20,16},{24,28},{28,24},{1,5},{5... | collective-permute-start | bytes 3551240 | tf_op jit(solution)/shard_map/ppermute | solution.py:94
  207.3 47.6 %collective-permute-start.53 = (bf16[2,2,136,1088]{3,2,1,0:T(8,128)(2,1)S(1)}, bf16[2,2,136,1088]{3,2,1,0:T(8,128)(2,1)S(1)}, u32[]{:S(2)}, u32[]{:S(2)}) collective-permute-start(bf16[2,2,136,1088]{3,2,1,0:T(8,128)(2,1)S(1)} %dynamic-slice_bitcast_fusion.1), channel_id=1, source_target_pairs={{0,8},{4,12},{8,0},{12,4},{16,24},{20,28},{24,16},{28,20},{1,9},{5... | collective-permute-start | bytes 3551240 | tf_op jit(solution)/shard_map/ppermute | solution.py:94
  209.5 26.7 %collective-permute-start.19 = (bf16[256,1088]{0,1:T(8,128)(2,1)S(1)}, bf16[256,1088]{0,1:T(8,128)(2,1)S(1)}, u32[]{:S(2)}, u32[]{:S(2)}) collective-permute-start(bf16[256,1088]{0,1:T(8,128)(2,1)S(1)} %slice.434), channel_id=1, source_target_pairs={{0,2},{1,3},{2,0},{3,1},{4,6},{5,7},{6,4},{7,5},{8,10},{9,11},{10,... | collective-permute-start | bytes 1671176 | tf_op jit(solution)/shard_map/ppermute | solution.py:46
  235.5 47.1 %collective-permute-start.15 = (bf16[256,1088]{0,1:T(8,128)(2,1)S(1)}, bf16[256,1088]{0,1:T(8,128)(2,1)S(1)}, u32[]{:S(2)}, u32[]{:S(2)}) collective-permute-start(bf16[256,1088]{0,1:T(8,128)(2,1)S(1)} %slice.435), channel_id=1, source_target_pairs={{0,2},{1,3},{2,0},{3,1},{4,6},{5,7},{6,4},{7,5},{8,10},{9,11},{10,... | collective-permute-start | bytes 1671176 | tf_op jit(solution)/shard_map/ppermute | solution.py:46
  236.2 15.6 %collective-permute-start.60 = (bf16[2,136,1088]{2,1,0:T(8,128)(2,1)S(1)}, bf16[2,136,1088]{2,1,0:T(8,128)(2,1)S(1)}, u32[]{:S(2)}, u32[]{:S(2)}) collective-permute-start(bf16[2,136,1088]{2,1,0:T(8,128)(2,1)S(1)} %dynamic-slice_bitcast_fusion.2), channel_id=1, source_target_pairs={{0,8},{4,12},{8,0},{12,4},{16,24},{20,28},{24,16},{28,20},{1,9},{5... | collective-permute-start | bytes 1775624 | tf_op jit(solution)/shard_map/ppermute | solution.py:94
  252.1 30.4 %collective-permute-start.61 = (bf16[136,1088]{1,0:T(8,128)(2,1)S(1)}, bf16[136,1088]{1,0:T(8,128)(2,1)S(1)}, u32[]{:S(2)}, u32[]{:S(2)}) collective-permute-start(bf16[136,1088]{1,0:T(8,128)(2,1)S(1)} %dynamic-slice_bitcast_fusion.6), channel_id=1, source_target_pairs={{0,16},{4,20},{8,24},{12,28},{16,0},{20,4},{24,8},{28,12},{1,17},{... | collective-permute-start | bytes 887816 | tf_op jit(solution)/shard_map/ppermute | solution.py:94
  255.3 52.9 %collective-permute-start.54 = (bf16[2,136,1088]{2,1,0:T(8,128)(2,1)S(1)}, bf16[2,136,1088]{2,1,0:T(8,128)(2,1)S(1)}, u32[]{:S(2)}, u32[]{:S(2)}) collective-permute-start(bf16[2,136,1088]{2,1,0:T(8,128)(2,1)S(1)} %dynamic-slice_bitcast_fusion.3), channel_id=1, source_target_pairs={{0,16},{4,20},{8,24},{12,28},{16,0},{20,4},{24,8},{28,12},{1,17},{... | collective-permute-start | bytes 1775624 | tf_op jit(solution)/shard_map/ppermute | solution.py:94
  282.6 25.6 %collective-permute-start.62 = (bf16[136,1088]{1,0:T(8,128)(2,1)S(1)}, bf16[136,1088]{1,0:T(8,128)(2,1)S(1)}, u32[]{:S(2)}, u32[]{:S(2)}) collective-permute-start(bf16[136,1088]{1,0:T(8,128)(2,1)S(1)} %fusion.47), channel_id=1, source_target_pairs={{0,16},{4,20},{8,24},{12,28},{16,0},{20,4},{24,8},{28,12},{1,17},{... | collective-permute-start | bytes 887816 | tf_op jit(solution)/shard_map/ppermute | solution.py:94
  284.6 26.3 %collective-permute-start.22 = (bf16[256,1088]{0,1:T(8,128)(2,1)S(1)}, bf16[256,1088]{0,1:T(8,128)(2,1)S(1)}, u32[]{:S(2)}, u32[]{:S(2)}) collective-permute-start(bf16[256,1088]{0,1:T(8,128)(2,1)S(1)} %get-tuple-element.47), channel_id=1, source_target_pairs={{0,2},{1,3},{2,0},{3,1},{4,6},{5,7},{6,4},{7,5},{8,10},{9,11},{10,... | collective-permute-start | bytes 1671176 | tf_op jit(solution)/shard_map/ppermute | solution.py:46
  310.2 14.8 %collective-permute-start.63 = (bf16[2,136,1088]{2,1,0:T(8,128)(2,1)S(1)}, bf16[2,136,1088]{2,1,0:T(8,128)(2,1)S(1)}, u32[]{:S(2)}, u32[]{:S(2)}) collective-permute-start(bf16[2,136,1088]{2,1,0:T(8,128)(2,1)S(1)} %pad_maximum_fusion.20), channel_id=1, source_target_pairs={{0,8},{4,12},{8,0},{12,4},{16,24},{20,28},{24,16},{28,20},{1,9},{5... | collective-permute-start | bytes 1775624 | tf_op jit(solution)/shard_map/ppermute | solution.py:94
  311.0 20.9 %collective-permute-start.23 = (bf16[512,1088]{0,1:T(8,128)(2,1)S(1)}, bf16[512,1088]{0,1:T(8,128)(2,1)S(1)}, u32[]{:S(2)}, u32[]{:S(2)}) collective-permute-start(bf16[512,1088]{0,1:T(8,128)(2,1)S(1)} %pad_maximum_fusion.13), channel_id=1, source_target_pairs={{0,1},{1,0},{2,3},{3,2},{4,5},{5,4},{6,7},{7,6},{8,9},{9,8},{10,11... | collective-permute-start | bytes 3342344 | tf_op jit(solution)/shard_map/ppermute | solution.py:46
  326.3 86.0 %collective-permute-start.64 = (bf16[2,2,136,1088]{3,2,1,0:T(8,128)(2,1)}, bf16[2,2,136,1088]{3,2,1,0:T(8,128)(2,1)}, u32[]{:S(2)}, u32[]{:S(2)}) collective-permute-start(bf16[2,2,136,1088]{3,2,1,0:T(8,128)(2,1)} %pad_maximum_fusion.9), channel_id=1, source_target_pairs={{0,4},{4,0},{8,12},{12,8},{16,20},{20,16},{24,28},{28,24},{1,5},{5... | collective-permute-start | bytes 3551240 | tf_op jit(solution)/shard_map/ppermute | solution.py:94
  328.5 35.3 %collective-permute-start.57 = (bf16[2,136,1088]{2,1,0:T(8,128)(2,1)}, bf16[2,136,1088]{2,1,0:T(8,128)(2,1)}, u32[]{:S(2)}, u32[]{:S(2)}) collective-permute-start(bf16[2,136,1088]{2,1,0:T(8,128)(2,1)} %pad_maximum_fusion.19), channel_id=1, source_target_pairs={{0,16},{4,20},{8,24},{12,28},{16,0},{20,4},{24,8},{28,12},{1,17},{... | collective-permute-start | bytes 1775624 | tf_op jit(solution)/shard_map/ppermute | solution.py:94
  350.1 86.8 %collective-permute-start.24 = (bf16[512,1088]{0,1:T(8,128)(2,1)}, bf16[512,1088]{0,1:T(8,128)(2,1)}, u32[]{:S(2)}, u32[]{:S(2)}) collective-permute-start(bf16[512,1088]{0,1:T(8,128)(2,1)} %slice.429), channel_id=1, source_target_pairs={{0,1},{1,0},{2,3},{3,2},{4,5},{5,4},{6,7},{7,6},{8,9},{9,8},{10,11... | collective-permute-start | bytes 3342344 | tf_op jit(solution)/shard_map/ppermute | solution.py:46
  360.9 12.6 %collective-permute-start.31 = (bf16[1,272,816]{2,1,0:T(8,128)(2,1)S(1)}, bf16[1,272,816]{2,1,0:T(8,128)(2,1)S(1)}, u32[]{:S(2)}, u32[]{:S(2)}) collective-permute-start(bf16[1,272,816]{2,1,0:T(8,128)(2,1)S(1)} %get-tuple-element.81), channel_id=1, source_target_pairs={{0,1},{1,0},{2,3},{3,2},{4,5},{5,4},{6,7},{7,6},{8,9},{9,8},{10,11... | collective-permute-start | bytes 1331720 | tf_op jit(solution)/shard_map/ppermute | solution.py:46
  361.0 14.3 %collective-permute-start.32 = (bf16[1,272,816]{2,1,0:T(8,128)(2,1)S(1)}, bf16[1,272,816]{2,1,0:T(8,128)(2,1)S(1)}, u32[]{:S(2)}, u32[]{:S(2)}) collective-permute-start(bf16[1,272,816]{2,1,0:T(8,128)(2,1)S(1)} %get-tuple-element.80), channel_id=1, source_target_pairs={{0,2},{1,3},{2,0},{3,1},{4,6},{5,7},{6,4},{7,5},{8,10},{9,11},{10,... | collective-permute-start | bytes 1331720 | tf_op jit(solution)/shard_map/ppermute | solution.py:46
  373.4 12.9 %collective-permute-start.33 = (bf16[1,272,816]{2,1,0:T(8,128)(2,1)S(1)}, bf16[1,272,816]{2,1,0:T(8,128)(2,1)S(1)}, u32[]{:S(2)}, u32[]{:S(2)}) collective-permute-start(bf16[1,272,816]{2,1,0:T(8,128)(2,1)S(1)} %get-tuple-element.79), channel_id=1, source_target_pairs={{0,3},{1,2},{2,1},{3,0},{4,7},{5,6},{6,5},{7,4},{8,11},{9,10},{10,... | collective-permute-start | bytes 1331720 | tf_op jit(solution)/shard_map/ppermute | solution.py:46
  373.5 87.5 %collective-permute-start.58 = (bf16[2,2,136,1088]{3,2,1,0:T(8,128)(2,1)S(1)}, bf16[2,2,136,1088]{3,2,1,0:T(8,128)(2,1)S(1)}, u32[]{:S(2)}, u32[]{:S(2)}) collective-permute-start(bf16[2,2,136,1088]{3,2,1,0:T(8,128)(2,1)S(1)} %pad_maximum_fusion.8), channel_id=1, source_target_pairs={{0,8},{4,12},{8,0},{12,4},{16,24},{20,28},{24,16},{28,20},{1,9},{5... | collective-permute-start | bytes 3551240 | tf_op jit(solution)/shard_map/ppermute | solution.py:94
  375.3 35.3 %collective-permute-start.47 = (bf16[136,1088]{1,0:T(8,128)(2,1)S(1)}, bf16[136,1088]{1,0:T(8,128)(2,1)S(1)}, u32[]{:S(2)}, u32[]{:S(2)}) collective-permute-start(bf16[136,1088]{1,0:T(8,128)(2,1)S(1)} %fusion.49), channel_id=1, source_target_pairs={{0,8},{4,12},{8,0},{12,4},{16,24},{20,28},{24,16},{28,20},{1,9},{5... | collective-permute-start | bytes 887816 | tf_op jit(solution)/shard_map/ppermute | solution.py:94
  386.6 43.6 %collective-permute-start.40 = (bf16[2,2,136,432]{3,2,1,0:T(8,128)(2,1)S(1)}, bf16[2,2,136,432]{3,2,1,0:T(8,128)(2,1)S(1)}, u32[]{:S(2)}, u32[]{:S(2)}) collective-permute-start(bf16[2,2,136,432]{3,2,1,0:T(8,128)(2,1)S(1)} %dynamic-slice_bitcast_fusion.4), channel_id=1, source_target_pairs={{0,8},{4,12},{8,0},{12,4},{16,24},{20,28},{24,16},{28,20},{1,9},{5... | collective-permute-start | bytes 1410056 | tf_op jit(solution)/shard_map/ppermute | solution.py:94
  412.3 16.3 %collective-permute-start.48 = (bf16[136,1088]{1,0:T(8,128)(2,1)S(1)}, bf16[136,1088]{1,0:T(8,128)(2,1)S(1)}, u32[]{:S(2)}, u32[]{:S(2)}) collective-permute-start(bf16[136,1088]{1,0:T(8,128)(2,1)S(1)} %add_convert_fusion.3), channel_id=1, source_target_pairs={{0,16},{4,20},{8,24},{12,28},{16,0},{20,4},{24,8},{28,12},{1,17},{... | collective-permute-start | bytes 887816 | tf_op jit(solution)/shard_map/ppermute | solution.py:94
  422.2 11.7 %collective-permute-start.35 = (bf16[2,136,384]{2,1,0:T(8,128)(2,1)S(1)}, bf16[2,136,384]{2,1,0:T(8,128)(2,1)S(1)}, u32[]{:S(2)}, u32[]{:S(2)}) collective-permute-start(bf16[2,136,384]{2,1,0:T(8,128)(2,1)S(1)} %dynamic-slice_bitcast_fusion.10), channel_id=1, source_target_pairs={{0,8},{4,12},{8,0},{12,4},{16,24},{20,28},{24,16},{28,20},{1,9},{5... | collective-permute-start | bytes 626696 | tf_op jit(solution)/shard_map/ppermute | solution.py:94
  428.7 22.1 %collective-permute-start.49 = (bf16[136,1088]{1,0:T(8,128)(2,1)S(1)}, bf16[136,1088]{1,0:T(8,128)(2,1)S(1)}, u32[]{:S(2)}, u32[]{:S(2)}) collective-permute-start(bf16[136,1088]{1,0:T(8,128)(2,1)S(1)} %add_convert_fusion.2), channel_id=1, source_target_pairs={{0,4},{4,0},{8,12},{12,8},{16,20},{20,16},{24,28},{28,24},{1,5},{5... | collective-permute-start | bytes 887816 | tf_op jit(solution)/shard_map/ppermute | solution.py:94
  430.4 18.6 %collective-permute-start.41 = (bf16[2,136,432]{2,1,0:T(8,128)(2,1)S(1)}, bf16[2,136,432]{2,1,0:T(8,128)(2,1)S(1)}, u32[]{:S(2)}, u32[]{:S(2)}) collective-permute-start(bf16[2,136,432]{2,1,0:T(8,128)(2,1)S(1)} %dynamic-slice_bitcast_fusion.9), channel_id=1, source_target_pairs={{0,16},{4,20},{8,24},{12,28},{16,0},{20,4},{24,8},{28,12},{1,17},{... | collective-permute-start | bytes 705032 | tf_op jit(solution)/shard_map/ppermute | solution.py:94
  434.0 16.7 %collective-permute-start.36 = (bf16[136,384]{1,0:T(8,128)(2,1)S(1)}, bf16[136,384]{1,0:T(8,128)(2,1)S(1)}, u32[]{:S(2)}, u32[]{:S(2)}) collective-permute-start(bf16[136,384]{1,0:T(8,128)(2,1)S(1)} %dynamic-slice_bitcast_fusion.12), channel_id=1, source_target_pairs={{0,16},{4,20},{8,24},{12,28},{16,0},{20,4},{24,8},{28,12},{1,17},{... | collective-permute-start | bytes 313352 | tf_op jit(solution)/shard_map/ppermute | solution.py:94
  439.5 32.7 %collective-permute-start.25 = (bf16[256,1088]{0,1:T(8,128)(2,1)}, bf16[256,1088]{0,1:T(8,128)(2,1)}, u32[]{:S(2)}, u32[]{:S(2)}) collective-permute-start(bf16[256,1088]{0,1:T(8,128)(2,1)} %slice.433), channel_id=1, source_target_pairs={{0,2},{1,3},{2,0},{3,1},{4,6},{5,7},{6,4},{7,5},{8,10},{9,11},{10,... | collective-permute-start | bytes 1671176 | tf_op jit(solution)/shard_map/ppermute | solution.py:46
  457.8 11.7 %collective-permute-start.38 = (bf16[2,136,384]{2,1,0:T(8,128)(2,1)}, bf16[2,136,384]{2,1,0:T(8,128)(2,1)}, u32[]{:S(2)}, u32[]{:S(2)}) collective-permute-start(bf16[2,136,384]{2,1,0:T(8,128)(2,1)} %pad_maximum_fusion.28), channel_id=1, source_target_pairs={{0,8},{4,12},{8,0},{12,4},{16,24},{20,28},{24,16},{28,20},{1,9},{5... | collective-permute-start | bytes 626696 | tf_op jit(solution)/shard_map/ppermute | solution.py:94
  460.2 15.6 %collective-permute-start.44 = (bf16[2,136,432]{2,1,0:T(8,128)(2,1)}, bf16[2,136,432]{2,1,0:T(8,128)(2,1)}, u32[]{:S(2)}, u32[]{:S(2)}) collective-permute-start(bf16[2,136,432]{2,1,0:T(8,128)(2,1)} %pad_maximum_fusion.23), channel_id=1, source_target_pairs={{0,16},{4,20},{8,24},{12,28},{16,0},{20,4},{24,8},{28,12},{1,17},{... | collective-permute-start | bytes 705032 | tf_op jit(solution)/shard_map/ppermute | solution.py:94
  471.4 29.5 %collective-permute-start.39 = (bf16[2,2,136,384]{3,2,1,0:T(8,128)(2,1)}, bf16[2,2,136,384]{3,2,1,0:T(8,128)(2,1)}, u32[]{:S(2)}, u32[]{:S(2)}) collective-permute-start(bf16[2,2,136,384]{3,2,1,0:T(8,128)(2,1)} %pad_maximum_fusion.22), channel_id=1, source_target_pairs={{0,4},{4,0},{8,12},{12,8},{16,20},{20,16},{24,28},{28,24},{1,5},{5... | collective-permute-start | bytes 1253384 | tf_op jit(solution)/shard_map/ppermute | solution.py:94
  478.8 23.3 %collective-permute-start.45 = (bf16[2,2,136,432]{3,2,1,0:T(8,128)(2,1)}, bf16[2,2,136,432]{3,2,1,0:T(8,128)(2,1)S(1)}, u32[]{:S(2)}, u32[]{:S(2)}) collective-permute-start(bf16[2,2,136,432]{3,2,1,0:T(8,128)(2,1)} %pad_maximum_fusion.21), channel_id=1, source_target_pairs={{0,8},{4,12},{8,0},{12,4},{16,24},{20,28},{24,16},{28,20},{1,9},{5... | collective-permute-start | bytes 1410056 | tf_op jit(solution)/shard_map/ppermute | solution.py:94
  (71 other events, 808.9 us)
